TPU v7x, 256 devices: a whole 4x4x8 slice. The times are simulated.
256 devices in a mesh: wide: 16 (over y, z_lo, core), narrow: 16 (over z_hi, x).
Axes of the slice: x: 4, y: 4, z: 8 (z_hi: 4, z_lo: 2; z = z_hi * 2 + z_lo), core: 2. Of those that a mesh axis runs over, the one named last changes fastest.
Arguments:
- snapshots: bfloat16 [786432, 512], P(('wide', 'narrow')), as said below
- range_test: bfloat16 [512, 384], replicated, may hold values from -0.25 to 0.25
- corange_test: bfloat16 [786432, 768], P(('wide', 'narrow')), may hold values from -0.02734375 to 0.02734375
Outputs:
- basis: float32 [786432, 384], P(('wide', 'narrow'))
- cosketch: float32 [768, 512], P('wide', 'narrow')
Inputs may be any that keep to these rules, and one draw needn't show every extreme that they name: `snapshots`: snapshot values are finite and of order one to some tens.
All inputs are finite; a program needn't handle non-finite values.
Results may differ from a plain program's by a relative error of at most 0.0003.
Values sent between devices are 32-bit elements; how exact they have to be, the bound alone decides.
No kernel may reach another device: no remote copies, remote signals or barrier semaphores. Data moves between devices by JAX's collectives and lax.ppermute only.
A program may use at most 128 MiB of HBM per device.

v0:
```python
import jax
import jax.numpy as jnp
from jax import lax
from jax.sharding import PartitionSpec as P


def per_device(snapshots, range_test, corange_test):
    rows = snapshots.shape[0]
    n_wide = lax.axis_size("wide")
    n_narrow = lax.axis_size("narrow")
    sketch = jnp.dot(snapshots, range_test, preferred_element_type=jnp.float32)
    gram = jnp.dot(sketch.T, sketch, precision=lax.Precision.HIGHEST)
    inner = lax.psum(gram, "narrow")
    lower = jnp.linalg.cholesky(lax.psum(inner, "wide"))
    contract = (((0,), (0,)), ((), ()))
    shares = lax.psum_scatter(
        lax.dot_general(corange_test, snapshots, contract, preferred_element_type=jnp.float32),
        "wide",
        scatter_dimension=0,
        tiled=True,
    )
    cosketch = lax.psum_scatter(shares, "narrow", scatter_dimension=1, tiled=True)
    solved = lax.linalg.triangular_solve(
        lower, sketch, left_side=False, lower=True, transpose_a=True
    )
    total = rows * n_wide * n_narrow
    basis = solved * jnp.sqrt(jnp.float32(total))
    return (basis, cosketch)


def solution(mesh):
    in_specs = (P(("wide", "narrow"), None), P(), P(("wide", "narrow"), None))
    out_specs = (P(("wide", "narrow"), None), P("wide", "narrow"))
    return jax.shard_map(
        per_device, mesh=mesh, in_specs=in_specs, out_specs=out_specs, check_vma=False
    )
```

profile of v0, /device:TPU:1, one launch (start us, length us, event | category | flops | bytes accessed | tf_op | source)
XLA Modules:
  0.0 539.9 jit_solution(1885302769253730188)
XLA Ops:
  7.2 0.0 copy-start
  7.2 0.0 all-reduce.4.cloned.1.call-start
  7.2 1.8 copy-done
  9.1 2.8 fusion.19
  11.8 0.0 copy-start.1
  11.9 2.2 copy-done.1
  14.0 8.6 %fusion.20 = f32[384,384]{0,1:T(8,128)} fusion(f32[3072,384]{1,0:T(8,128)S(1)} %fusion.19), kind=kOutput, calls=%fused_computation.48 | convolution fusion | flops 5435817984 | bytes 5308416 | tf_op jit(solution)/shard_map/dot_general | solution.py:12
  22.7 0.0 all-reduce.4.cloned.1.call-update
  22.7 0.0 all-reduce.6.cloned.1.call-start
  22.7 160.4 %all-reduce.4.cloned.1.call-done = f32[384,384]{0,1:T(8,128)} async-done(((f32[384,384]{0,1:T(8,128)}), f32[384,384]{0,1:T(8,128)}) %all-reduce.4.cloned.1.call-update) | async-done | bytes 589840 | tf_op jit(solution)/shard_map/psum | solution.py:13
  183.1 0.0 all-reduce.6.cloned.1.call-update
  183.2 0.0 reduce-scatter.5.cloned.1.call-start
  183.2 6.1 %fusion.21 = f32[768,512]{1,0:T(8,128)} fusion(bf16[3072,768]{1,0:T(8,128)(2,1)} %param.5, bf16[3072,512]{1,0:T(8,128)(2,1)S(1)} %copy-done), kind=kOutput, calls=%fused_computation.49 | convolution fusion | flops 2415919104 | bytes 9437184 | tf_op jit(solution)/shard_map/dot_general | solution.py:17
  189.3 0.0 reduce-scatter.5.cloned.1.call-update
  189.3 0.3 reduce-scatter.7.cloned.1.call-start
  189.6 124.4 %all-reduce.6.cloned.1.call-done = f32[384,384]{0,1:T(8,128)} async-done(((f32[384,384]{0,1:T(8,128)}), f32[384,384]{0,1:T(8,128)}) %all-reduce.6.cloned.1.call-update) | async-done | bytes 589840 | tf_op jit(solution)/shard_map/psum | solution.py:14
  314.0 2.1 copy.10
  316.1 1.3 fusion.5
  317.4 0.0 copy-start.4
  317.4 0.8 copy-done.4
  318.2 11.7 %cholesky.77 = f32[128,128]{1,0:T(8,128)S(1)} custom-call(f32[128,128]{1,0:T(8,128)S(1)} %cholesky.192), custom_call_target="Cholesky" | custom-call | tf_op jit(solution)/shard_map/jit(cholesky)/cholesky | solution.py:14
  330.0 9.8 %custom-call.22 = f32[1,128,128]{1,2,0:T(8,128)S(1)} custom-call(f32[1,128,128]{2,1,0:T(8,128)S(1)} %get-tuple-element.30), custom_call_target="InvertDiagBlocksLowerTriangular" | custom-call | tf_op jit(solution)/shard_map/jit(cholesky)/cholesky | solution.py:14
  339.8 0.9 cholesky.169
  340.7 1.9 constant_dynamic-update-slice_fusion.2
  342.5 1.2 convolution_subtract_fusion.2
  343.7 11.7 %cholesky.162 = f32[128,128]{1,0:T(8,128)S(1)} custom-call(f32[128,128]{1,0:T(8,128)S(1)} %cholesky.196), custom_call_target="Cholesky" | custom-call | tf_op jit(solution)/shard_map/jit(cholesky)/cholesky | solution.py:14
  355.4 0.6 select_reduce_fusion.1
  356.1 10.2 %custom-call.23 = f32[1,128,128]{1,2,0:T(8,128)S(1)} custom-call(f32[1,128,128]{2,1,0:T(8,128)S(1)} %get-tuple-element.27), custom_call_target="InvertDiagBlocksLowerTriangular" | custom-call | tf_op jit(solution)/shard_map/jit(cholesky)/cholesky | solution.py:14
  366.2 0.8 convolution_dynamic-update-slice_fusion
  367.1 1.3 convolution_subtract_fusion.3
  368.3 11.7 %cholesky.181 = f32[128,128]{1,0:T(8,128)S(1)} custom-call(f32[128,128]{1,0:T(8,128)S(1)} %convolution_subtract_fusion.3), custom_call_target="Cholesky" | custom-call | tf_op jit(solution)/shard_map/jit(cholesky)/cholesky | solution.py:14
  380.0 0.7 compare_reduce_fusion.1
  382.0 0.6 select_reduce_fusion
  382.6 0.7 compare_reduce_fusion
  383.9 1.9 select_select_fusion
  385.9 10.5 %while.1 = (s32[]{:T(128)}, f32[384,384]{1,0:T(8,128)}, s32[3,2]{0,1:T(2,128)S(1)}, f32[3,128,128]{2,1,0:T(8,128)}, s32[]{:T(128)}) while((s32[]{:T(128)}, f32[384,384]{1,0:T(8,128)}, s32[3,2]{0,1:T(2,128)S(1)}, f32[3,128,128]{2,1,0:T(8,128)}, s32[]{:T(128)}) %tuple.31), condition=%wide.while_cond, body=%wide.while_body.sunk | while | flops 2 | bytes 132705 | solution.py:23
  385.9 0.1 constant_dynamic-slice_fusion.2
  385.9 0.6 fusion.33
  386.5 2.9 bitcast_dynamic-update-slice_fusion.2
  389.4 0.1 constant_dynamic-slice_fusion.2
  389.4 0.6 fusion.33
  390.0 2.9 bitcast_dynamic-update-slice_fusion.2
  392.9 0.1 constant_dynamic-slice_fusion.2
  393.0 0.6 fusion.33
  393.5 2.8 bitcast_dynamic-update-slice_fusion.2
  396.3 30.5 %custom-call.24 = f32[3,128,128]{1,2,0:T(8,128)S(1)} custom-call(f32[3,128,128]{2,1,0:T(8,128)} %get-tuple-element.9), custom_call_target="InvertDiagBlocksLowerTriangular" | custom-call | tf_op jit(solution)/shard_map/triangular_solve | solution.py:23
  426.8 3.0 fusion.3
  429.8 0.0 copy-start.2
  429.8 4.7 convolution_subtract_fusion
  434.5 1.6 fusion.11
  436.1 0.0 copy-done.2
  436.1 0.0 copy-start.3
  436.1 7.4 %convolution_subtract_fusion.1 = f32[3072,128]{1,0:T(8,128)S(1)} fusion(f32[3072,128]{0,1:T(8,128)S(1)} %fusion.11, f32[3072,128]{0,1:T(8,128)S(1)} %fusion.3, f32[3072,384]{1,0:T(8,128)} %copy-done.1, f32[384,384]{1,0:T(8,128)} %get-tuple-element.86), kind=kOutput, calls=%fused_computation.4 | convolution fusion | flops 1209139200 | bytes 6422528 | tf_op jit(solution)/shard_map/triangular_solve | solution.py:23
  443.5 0.0 copy-done.3
  443.5 2.7 fusion.10
  446.2 0.0 reduce-scatter.5.cloned.1.call-done
  446.2 1.7 copy.14
  447.9 0.0 reduce-scatter.7.cloned.1.call-update
  447.9 5.2 maximum_multiply_fusion
  453.2 6.0 %copy.11 = f32[3072,384]{1,0:T(8,128)} copy(f32[3072,384]{0,1:T(8,128)} %maximum_multiply_fusion) | data formatting | bytes 9437184
  459.2 73.9 %reduce-scatter.7.cloned.1.call-done = f32[32,48]{1,0:T(8,128)} async-done(((f32[512,48]{1,0:T(8,128)}), f32[32,48]{1,0:T(8,128)}) %reduce-scatter.7.cloned.1.call-update) | async-done | bytes 6160
  (6 shorter events, 0.1 us)
Async XLA Ops:
  7.2 1.9 copy-start
  7.2 176.0 %all-reduce.4.cloned.1.call-start = ((), (), s32[]{:S(2)}) async-start(), calls=%async_computation.2 | async-start | bytes 1179648 | tf_op jit(solution)/shard_map/psum | solution.py:13
  11.8 2.2 copy-start.1
  22.7 291.3 %all-reduce.6.cloned.1.call-start = ((), (), s32[]{:S(2)}) async-start(), calls=%async_computation.3 | async-start | bytes 1179648 | tf_op jit(solution)/shard_map/psum | solution.py:14
  183.2 263.0 %reduce-scatter.5.cloned.1.call-start = ((), (), s32[]{:S(2)}) async-start(), calls=%async_computation.4 | async-start | bytes 1671168 | tf_op jit(solution)/shard_map/reduce_scatter | solution.py:16
  189.3 343.8 %reduce-scatter.7.cloned.1.call-start = ((), (), s32[]{:S(2)}) async-start(), calls=%async_computation.5 | async-start | bytes 278528
  317.4 0.8 copy-start.4
  429.8 6.3 %copy-start.2 = (f32[3072,128]{0,1:T(8,128)}, f32[3072,128]{0,1:T(8,128)S(1)}, u32[]{:S(2)}) copy-start(f32[3072,128]{0,1:T(8,128)S(1)} %fusion.3) | copy-start | bytes 4718596
  436.1 7.4 %copy-start.3 = (f32[3072,128]{0,1:T(8,128)}, f32[3072,128]{0,1:T(8,128)S(1)}, u32[]{:S(2)}) copy-start(f32[3072,128]{0,1:T(8,128)S(1)} %fusion.11) | copy-start | bytes 4718596
Sparse Core Ops, SparseCore 0:
  22.8 160.2 all-reduce.3
  185.9 128.0 all-reduce.5
  316.5 64.1 reduce-scatter.4
  448.1 85.0 reduce-scatter.6
where the time goes:
time: 550 us; the launch traced here: 540 us
  waiting for transfers between devices  359 us (65%)
  other arithmetic  96.7 us (18%)
  matrix products  42 us (8%)
  local copies, waits for them, and re-layouts  26.1 us (5%)
  between operations  16 us (3%)
    psum x1, waiting for transfers between devices, per_device(): inner = lax.psum(gram, 'narrow')  160 us
    psum x1, waiting for transfers between devices, per_device(): lower = jnp.linalg.cholesky(lax.psum(inner, 'wide'))  124 us
    unnamed x5, waiting for transfers between devices  74 us
    another operation x10, other arithmetic, per_device(): lower = jnp.linalg.cholesky(lax.psum(inner, 'wide'))  57.8 us
    another operation x3, other arithmetic, per_device(): lax.linalg.triangular_solve(lower, sketch, left_side=False, lower=True, t...  32.4 us
    another operation x5, matrix products, per_device(): lax.linalg.triangular_solve(lower, sketch, left_side=False, lower=True, t...  19.3 us
    unnamed x12, local copies, waits for them, and re-layouts  12.6 us
  transfers between devices with their start and end apart: 4, of which 3 were waited for; matrix products, arithmetic and copies ran while one was open for 27% of the time, Pallas kernels for 0%

commit v1 on v0

v1 whole, which is shorter than its diff:
```python
import jax
import jax.numpy as jnp
from jax import lax
from jax.experimental import pallas as pl
from jax.experimental.pallas import tpu as pltpu
from jax.sharding import Mesh, PartitionSpec as P

F32 = jnp.float32
BF16 = jnp.bfloat16
ROWS = ("y", "zl", "core", "zh", "x")
PLANE = ("y", "x")
COLUMN = ("zl", "zh")
VMEM = pl.BlockSpec(memory_space=pltpu.VMEM)
ANY = pl.BlockSpec(memory_space=pl.ANY)
CONTRACT0 = (((0,), (0,)), ((), ()))
BLOCKS = ((0, 0), (0, 1), (0, 2), (1, 1), (1, 2), (2, 2))


def split(value, parts):
    pieces = []
    for _ in range(parts):
        piece = value.astype(BF16)
        pieces.append(piece)
        value = value - piece.astype(F32)
    return pieces


def lanes(shape):
    return lax.broadcasted_iota(jnp.int32, shape, len(shape) - 1)


def products_kernel(x_ref, c_ref, r_ref, mine_ref, other_ref, s_acc, k_acc, g_acc, p_acc):
    step = pl.program_id(0)
    x = x_ref[...]
    s = lax.dot_general(x, x, CONTRACT0, preferred_element_type=F32)
    k = lax.dot_general(c_ref[...], x, CONTRACT0, preferred_element_type=F32)

    @pl.when(step == 0)
    def _():
        s_acc[...] = s
        k_acc[...] = k

    @pl.when(step > 0)
    def _():
        s_acc[...] += s
        k_acc[...] += k

    @pl.when(step == pl.num_programs(0) - 1)
    def _():
        r = r_ref[...]
        t = sum(jnp.dot(p, r, preferred_element_type=F32) for p in split(s_acc[...], 3))
        pieces = split(t, 3)
        at = 0
        for i in range(3):
            left = r[:, i * 128 : (i + 1) * 128]
            row = sum(
                lax.dot_general(left, p[:, i * 128 :], CONTRACT0, preferred_element_type=F32)
                for p in pieces
            )
            for j in range(3 - i):
                g_acc[at * 128 : (at + 1) * 128, :] = row[:, j * 128 : (j + 1) * 128]
                at += 1
        quarter = lanes((768, 128)) // 32
        for n in range(4):
            out = jnp.zeros((768, 128), F32)
            for zh in range(4):
                piece = k_acc[:, zh * 128 : (zh + 1) * 128]
                shift = ((zh - n) * 32) % 128
                if shift:
                    piece = pltpu.roll(piece, shift, 1)
                out = jnp.where(quarter == zh, piece, out)
            p_acc[n] = out
        core = lax.axis_index("core")
        for side, ref in ((core, mine_ref), (1 - core, other_ref)):
            for y in range(4):
                for n in range(4):
                    peer = y * 4 + n
                    ref[peer, 0:24, :] = g_acc[pl.ds(pl.multiple_of(side * 384 + peer * 24, 8), 24), :]
                    for zl in range(2):
                        start = pl.multiple_of((y * 4 + zl * 2 + side) * 48, 8)
                        ref[peer, 24 + zl * 48 : 72 + zl * 48, :] = p_acc[n, pl.ds(start, 48), :]


def products(x, c, r):
    tile = 1024
    half = jax.ShapeDtypeStruct((16, 120, 128), F32)
    whole = pl.BlockSpec((16, 120, 128), lambda i: (0, 0, 0))
    return pl.pallas_call(
        products_kernel,
        grid=(x.shape[0] // tile,),
        in_specs=[
            pl.BlockSpec((tile, 512), lambda i: (i, 0)),
            pl.BlockSpec((tile, 768), lambda i: (i, 0)),
            pl.BlockSpec((512, 384), lambda i: (0, 0)),
        ],
        out_specs=(whole, whole),
        out_shape=(half, half),
        scratch_shapes=[
            pltpu.VMEM((512, 512), F32),
            pltpu.VMEM((768, 512), F32),
            pltpu.VMEM((768, 128), F32),
            pltpu.VMEM((4, 768, 128), F32),
        ],
        compiler_params=pltpu.CompilerParams(vmem_limit_bytes=48 << 20),
    )(x, c, r)


def column_kernel(got_ref, out_ref):
    total = got_ref[0]
    for i in range(1, 16):
        total = total + got_ref[i]
    gram = total[0:24]
    lane = lanes((16, 128)) // 32
    for zl in range(2):
        for zh in range(4):
            peer = zl * 4 + zh
            out_ref[peer, 0:24, :] = gram
            out = jnp.zeros((16, 128), F32)
            for q in range(3):
                start = 24 + zl * 48 + q * 16
                piece = total[start : start + 16]
                shift = ((q - zh) * 32) % 128
                if shift:
                    piece = pltpu.roll(piece, shift, 1)
                out = jnp.where(lane == q, piece, out)
            out_ref[peer, 24:40, :] = out


def column_blocks(got):
    return pl.pallas_call(
        column_kernel,
        in_specs=[VMEM],
        out_specs=VMEM,
        out_shape=jax.ShapeDtypeStruct((8, 40, 128), F32),
    )(got)


def plane_kernel(got_ref, gram_ref, cosketch_ref):
    total = got_ref[0]
    for i in range(1, 8):
        total = total + got_ref[i]
    for i in range(16):
        gram_ref[i] = total[0:24]
    for q in range(3):
        piece = total[24:40]
        if q:
            piece = pltpu.roll(piece, 128 - q * 32, 1)
        cosketch_ref[q * 16 : (q + 1) * 16, :] = piece[:, 0:32]


def plane_blocks(got):
    return pl.pallas_call(
        plane_kernel,
        in_specs=[VMEM],
        out_specs=(VMEM, VMEM),
        out_shape=(
            jax.ShapeDtypeStruct((16, 24, 128), F32),
            jax.ShapeDtypeStruct((48, 32), F32),
        ),
    )(got)


def spread(value):
    return jnp.broadcast_to(value, (8, 128))


def inverse_factor(block):
    n = 16
    d = [block[8 * i : 8 * i + 8, :] for i in range(n)]
    row = lax.broadcasted_iota(jnp.int32, (8, 128), 0)
    lane = lanes((8, 128))
    v = [jnp.where(lane == row + 8 * i, 1.0, 0.0).astype(F32) for i in range(n)]
    for p in range(n):
        columns = [spread(d[p][:, 8 * p + j : 8 * p + j + 1]) for j in range(8)]
        s = [[spread(columns[j][k : k + 1, :]) if k >= j else None for j in range(8)] for k in range(8)]
        r = []
        for j in range(8):
            r.append(lax.rsqrt(s[j][j]))
            for k in range(j + 1, 8):
                s[k][j] = s[k][j] * r[j]
            for m in range(j + 1, 8):
                for k in range(m, 8):
                    s[k][m] = s[k][m] - s[k][j] * s[m][j]

        def forward(rows):
            done = []
            for j in range(8):
                value = rows[j]
                for i in range(j):
                    value = value - s[j][i] * done[i]
                done.append(value * r[j])
            return done

        vx = forward([spread(v[p][j : j + 1, :]) for j in range(8)])
        new = vx[0]
        for j in range(1, 8):
            new = jnp.where(row == j, vx[j], new)
        v[p] = new
        if p == n - 1:
            break
        dx = forward([spread(d[p][j : j + 1, :]) for j in range(8)])
        for k in range(p + 1, n):
            factors = forward([spread(d[k][:, 8 * p + j : 8 * p + j + 1]) for j in range(8)])
            for j in range(8):
                d[k] = d[k] - factors[j] * dx[j]
                v[k] = v[k] - factors[j] * vx[j]
    return jnp.concatenate(v, axis=0)


def exact(a, b, contract=(((1,), (0,)), ((), ()))):
    return lax.dot_general(a, b, contract, precision=lax.Precision.HIGHEST, preferred_element_type=F32)


def basis_kernel(scale, tiles, a_ref, b_ref, r_ref, x_hbm, out_hbm, g, v, x_vmem, out_vmem, in_sem, out_sem):
    load = pltpu.make_async_copy(x_hbm, x_vmem, in_sem)
    load.start()
    core = lax.axis_index("core")
    g[pl.ds(pl.multiple_of(core * 384, 8), 384), :] = a_ref[...]
    g[pl.ds(pl.multiple_of((1 - core) * 384, 8), 384), :] = b_ref[...]

    def block(i):
        return g[i * 128 : (i + 1) * 128, :]

    m0 = inverse_factor(block(0))
    row0 = exact(m0, jnp.concatenate([block(1), block(2)], axis=1))
    minus = exact(row0, row0, CONTRACT0)
    left = -exact(row0, m0, CONTRACT0)
    m1 = inverse_factor(block(3) - minus[:128, :128])
    row1 = exact(m1, block(4) - minus[:128, 128:])
    m2 = inverse_factor(block(5) - minus[128:, 128:] - exact(row1, row1, CONTRACT0))
    v[...] = jnp.zeros((384, 384), F32)
    v[0:128, 0:128] = m0
    v10 = exact(m1, left[:128])
    v[128:256, 0:128] = v10
    v[128:256, 128:256] = m1
    v[256:384, 0:128] = exact(m2, left[128:] - exact(row1, v10, CONTRACT0))
    v[256:384, 128:256] = exact(m2, -exact(row1, m1, CONTRACT0))
    v[256:384, 256:384] = m2

    r = r_ref[...]
    w = sum(
        lax.dot_general(r, p, (((1,), (1,)), ((), ())), preferred_element_type=F32)
        for p in split(v[...], 3)
    )
    high, low = split(w * scale, 2)
    load.wait()
    size = x_vmem.shape[0] // tiles
    stores = []
    for i in range(tiles):
        at = pl.ds(i * size, size)
        x = x_vmem[at, :]
        out_vmem[at, :] = jnp.dot(x, high, preferred_element_type=F32) + jnp.dot(
            x, low, preferred_element_type=F32
        )
        store = pltpu.make_async_copy(out_vmem.at[at, :], out_hbm.at[at, :], out_sem.at[i])
        store.start()
        stores.append(store)
    for store in stores:
        store.wait()


def basis_of(scale, a, b, r, x):
    tiles = 6
    return pl.pallas_call(
        lambda *refs: basis_kernel(scale, tiles, *refs),
        in_specs=[VMEM, VMEM, VMEM, ANY],
        out_specs=ANY,
        out_shape=jax.ShapeDtypeStruct((x.shape[0], 384), F32),
        scratch_shapes=[
            pltpu.VMEM((768, 128), F32),
            pltpu.VMEM((384, 384), F32),
            pltpu.VMEM(x.shape, BF16),
            pltpu.VMEM((x.shape[0], 384), F32),
            pltpu.SemaphoreType.DMA,
            pltpu.SemaphoreType.DMA((tiles,)),
        ],
        compiler_params=pltpu.CompilerParams(vmem_limit_bytes=48 << 20),
    )(a, b, r, x)


def per_device(snapshots, range_test, corange_test):
    total = snapshots.shape[0] * 256
    swap = [(0, 1), (1, 0)]
    mine, other = products(snapshots, corange_test, range_test)
    pair = mine + lax.ppermute(other, "core", swap)
    got = lax.all_to_all(pair, PLANE, 0, 0, tiled=True)
    got = lax.all_to_all(column_blocks(got), COLUMN, 0, 0, tiled=True)
    gram, cosketch = plane_blocks(got)
    half = lax.all_to_all(gram, PLANE, 0, 0, tiled=True).reshape(384, 128)
    basis = basis_of(float(total) ** 0.5, half, lax.ppermute(half, "core", swap), range_test, snapshots)
    return basis, cosketch


def solution(mesh):
    fine = Mesh(mesh.devices.reshape(4, 2, 2, 4, 4), ROWS)
    in_specs = (P(ROWS, None), P(), P(ROWS, None))
    out_specs = (P(ROWS, None), P(("y", "zl", "core"), ("zh", "x")))
    return jax.shard_map(
        per_device, mesh=fine, in_specs=in_specs, out_specs=out_specs, check_vma=False
    )
```

time: 550 us -> 97.6 us (0.18); the launches traced: 540 us -> 97.1 us
  waiting for transfers between devices: 359 us -> 2.2 us
  other arithmetic: 96.7 us -> 0.1 us
  blocking collectives: 0 us -> 47.4 us
  matrix products: 42 us -> 0 us
  Pallas kernels: 0 us -> 34.9 us
  local copies, waits for them, and re-layouts: 26.1 us -> 4.31 us
  between operations: 16 us -> 0.86 us
  starting transfers between devices: 0.37 us -> 7.37 us
    psum x2 -> x0, waiting for transfers between devices: 285 us -> none  [the longest x1 160 us: per_device(): inner = lax.psum(gram, 'narrow')]
    another operation x13 -> x0, other arithmetic: 90.2 us -> none  [the longest x10 57.8 us: per_device(): lower = jnp.linalg.cholesky(lax.psum(inner, 'wide'))]
    unnamed x5 -> x0, waiting for transfers between devices: 74 us -> none
    all_to_all x0 -> x3, blocking collectives: none -> 47.4 us  [the longest x1 20.6 us: per_device(): got = lax.all_to_all(pair, PLANE, 0, 0, tiled=True)]
    pallas_call x0 -> x4, Pallas kernels: none -> 34.9 us  [the longest x1 22.3 us: basis_of(): pl.pallas_call(lambda *refs: basis_kernel(scale, tiles, *refs), in_specs=...]
    another operation x9 -> x0, matrix products: 24.4 us -> none  [the longest x5 19.3 us: per_device(): lax.linalg.triangular_solve(lower, sketch, left_side=False, lower=True, t...]
    dot_general x3 -> x0, matrix products: 17.5 us -> none  [the longest x1 8.63 us: per_device(): gram = jnp.dot(sketch.T, sketch, precision=lax.Precision.HIGHEST)]
    another operation x13 -> x0, local copies, waits for them, and re-layouts: 11.3 us -> none
  transfers between devices with their start and end apart: 4 -> 2, of which waited for: 3 -> 1; matrix products, arithmetic and copies ran while one was open for 27% -> 1% of each run, Pallas kernels for 0% -> 0%
where the time goes in v1:
time: 97.6 us; the launch traced here: 97.1 us
  blocking collectives  47.4 us (49%)
  Pallas kernels  34.9 us (36%)
  starting transfers between devices  7.37 us (8%)
  local copies, waits for them, and re-layouts  4.31 us (4%)
  waiting for transfers between devices  2.2 us (2%)
    pallas_call x1, Pallas kernels, basis_of(): pl.pallas_call(lambda *refs: basis_kernel(scale, tiles, *refs), in_specs=...  22.3 us
    all_to_all x1, blocking collectives, per_device(): got = lax.all_to_all(pair, PLANE, 0, 0, tiled=True)  20.6 us
    all_to_all x1, blocking collectives, per_device(): got = lax.all_to_all(column_blocks(got), COLUMN, 0, 0, tiled=True)  15.4 us
    all_to_all x1, blocking collectives, per_device(): half = lax.all_to_all(gram, PLANE, 0, 0, tiled=True).reshape(384, 128)  11.4 us
    pallas_call x1, Pallas kernels, products(): pl.pallas_call(products_kernel, grid=(x.shape[0] // tile,), in_specs=[pl....  8.97 us
    unnamed x9, local copies, waits for them, and re-layouts  4.31 us
    ppermute x1, starting transfers between devices, per_device(): lax.ppermute(half, 'core', swap)  4.07 us
    ppermute x1, starting transfers between devices, per_device(): pair = mine + lax.ppermute(other, 'core', swap)  3.3 us
  transfers between devices with their start and end apart: 2, of which 1 were waited for; matrix products, arithmetic and copies ran while one was open for 1% of the time, Pallas kernels for 0%

profile of v1, /device:TPU:1, one launch (start us, length us, event | category | flops | bytes accessed | tf_op | source)
XLA Modules:
  0.0 97.1 jit_solution(2242033912589254246)
XLA Ops:
  0.6 0.0 copy-start
  0.6 1.9 %copy-done = bf16[3072,512]{1,0:T(8,128)(2,1)S(1)} copy-done((bf16[3072,512]{1,0:T(8,128)(2,1)S(1)}, bf16[3072,512]{1,0:T(8,128)(2,1)}, u32[]{:S(2)}) %copy-start) | copy-done | bytes 3145752
  2.5 0.0 copy-start.2
  2.5 1.0 %copy-done.2 = bf16[512,384]{1,0:T(8,128)(2,1)S(1)} copy-done((bf16[512,384]{1,0:T(8,128)(2,1)S(1)}, bf16[512,384]{1,0:T(8,128)(2,1)}, u32[]{:S(2)}) %copy-start.2) | copy-done | bytes 393240
  3.5 9.0 %shard_map.50 = (f32[16,120,128]{2,1,0:T(8,128)S(1)}, f32[16,120,128]{2,1,0:T(8,128)S(1)}) custom-call(bf16[3072,512]{1,0:T(8,128)(2,1)S(1)} %copy-done, bf16[3072,768]{1,0:T(8,128)(2,1)} %c_ref.1, bf16[512,384]{1,0:T(8,128)(2,1)S(1)} %copy-done.2), custom_call_target="tpu_custom_call" | custom-call | tf_op jit(solution)/shard_map/pallas_call | solution.py:88
  12.5 0.0 copy-start.1
  12.5 0.0 copy-start.3
  12.5 3.3 %collective-permute-start = (f32[16,120,128]{2,1,0:T(8,128)S(1)}, f32[16,120,128]{2,1,0:T(8,128)S(1)}, u32[]{:S(2)}, u32[]{:S(2)}) collective-permute-start(f32[16,120,128]{2,1,0:T(8,128)S(1)} %get-tuple-element.7), channel_id=1, source_target_pairs={{0,16},{16,0},{1,17},{17,1},{2,18},{18,2},{3,19},{19,3},{4,20},{20... | collective-permute-start | bytes 2949128 | tf_op jit(solution)/shard_map/ppermute | solution.py:285
  15.8 2.2 %collective-permute-done = f32[16,120,128]{2,1,0:T(8,128)S(1)} collective-permute-done((f32[16,120,128]{2,1,0:T(8,128)S(1)}, f32[16,120,128]{2,1,0:T(8,128)S(1)}, u32[]{:S(2)}, u32[]{:S(2)}) %collective-permute-start) | collective-permute-done | bytes 983072 | tf_op jit(solution)/shard_map/ppermute | solution.py:285
  18.0 0.1 add.3
  18.1 20.6 %all_to_all.15.got_ref = f32[16,120,128]{2,1,0:T(8,128)} all-to-all(f32[16,120,128]{2,1,0:T(8,128)S(1)} %add.3), channel_id=1, replica_groups=mesh['y'=4,'zl'=2,'core'=2,'zh'=4,'x'=4] {'y','x'}, dimensions={0} | all-to-all | bytes 1966080 | tf_op jit(solution)/shard_map/all_to_all | solution.py:286
  38.7 2.0 %shard_map.51 = f32[8,40,128]{2,1,0:T(8,128)} custom-call(f32[16,120,128]{2,1,0:T(8,128)} %all_to_all.15.got_ref), custom_call_target="tpu_custom_call" | custom-call | tf_op jit(solution)/shard_map/pallas_call | solution.py:130
  40.7 15.4 %all_to_all.16.got_ref = f32[8,40,128]{2,1,0:T(8,128)} all-to-all(f32[8,40,128]{2,1,0:T(8,128)} %shard_map.51), channel_id=1, replica_groups=mesh['y'=4,'zl'=2,'core'=2,'zh'=4,'x'=4] {'zl','zh'}, dimensions={0} | all-to-all | bytes 327680 | tf_op jit(solution)/shard_map/all_to_all | solution.py:287
  56.1 1.6 %shard_map.52 = (f32[16,24,128]{2,1,0:T(8,128)}, f32[48,32]{1,0:T(8,128)}) custom-call(f32[8,40,128]{2,1,0:T(8,128)} %all_to_all.16.got_ref), custom_call_target="tpu_custom_call" | custom-call | tf_op jit(solution)/shard_map/pallas_call | solution.py:152
  57.7 11.4 %all_to_all.17 = f32[16,24,128]{2,1,0:T(8,128)} all-to-all(f32[16,24,128]{2,1,0:T(8,128)} %get-tuple-element.8), channel_id=1, replica_groups=mesh['y'=4,'zl'=2,'core'=2,'zh'=4,'x'=4] {'y','x'}, dimensions={0} | all-to-all | bytes 393216 | tf_op jit(solution)/shard_map/all_to_all | solution.py:289
  69.1 4.1 %collective-permute-start.1 = (f32[384,128]{1,0:T(8,128)}, f32[384,128]{1,0:T(8,128)}, u32[]{:S(2)}, u32[]{:S(2)}) collective-permute-start(f32[384,128]{1,0:T(8,128)} %bitcast.refs_0_), channel_id=1, source_target_pairs={{0,16},{16,0},{1,17},{17,1},{2,18},{18,2},{3,19},{19,3},{4,20},{20... | collective-permute-start | bytes 589832 | tf_op jit(solution)/shard_map/ppermute | solution.py:290
  73.2 1.4 %copy.5 = f32[48,32]{0,1:T(8,128)} copy(f32[48,32]{1,0:T(8,128)} %get-tuple-element.11) | data formatting | bytes 12288
  74.6 0.0 collective-permute-done.1.refs_1_
  74.6 0.0 copy-done.1
  74.6 0.0 copy-done.3
  74.6 22.3 %shard_map.53 = f32[3072,384]{1,0:T(8,128)} custom-call(f32[384,128]{1,0:T(8,128)} %bitcast.refs_0_, f32[384,128]{1,0:T(8,128)} %collective-permute-done.1.refs_1_, bf16[512,384]{1,0:T(8,128)(2,1)S(1)} %copy-done.3, bf16[3072,512]{1,0:T(8,128)(2,1)S(1)} %copy-done.1), custom_call_target="tpu_custom_call" | custom-call | tf_op jit(solution)/shard_map/pallas_call | solution.py:264
Async XLA Ops:
  0.6 1.9 %copy-start = (bf16[3072,512]{1,0:T(8,128)(2,1)S(1)}, bf16[3072,512]{1,0:T(8,128)(2,1)}, u32[]{:S(2)}) copy-start(bf16[3072,512]{1,0:T(8,128)(2,1)} %refs_3_.1) | copy-start | bytes 9437188
  2.5 1.0 %copy-start.2 = (bf16[512,384]{1,0:T(8,128)(2,1)S(1)}, bf16[512,384]{1,0:T(8,128)(2,1)}, u32[]{:S(2)}) copy-start(bf16[512,384]{1,0:T(8,128)(2,1)} %refs_2_.1) | copy-start | bytes 1179652
  12.5 62.1 %copy-start.1 = (bf16[3072,512]{1,0:T(8,128)(2,1)S(1)}, bf16[3072,512]{1,0:T(8,128)(2,1)}, u32[]{:S(2)}) copy-start(bf16[3072,512]{1,0:T(8,128)(2,1)} %refs_3_.1) | copy-start | bytes 9437188
  12.5 62.1 %copy-start.3 = (bf16[512,384]{1,0:T(8,128)(2,1)S(1)}, bf16[512,384]{1,0:T(8,128)(2,1)}, u32[]{:S(2)}) copy-start(bf16[512,384]{1,0:T(8,128)(2,1)} %refs_2_.1) | copy-start | bytes 1179652
  12.5 5.5 %collective-permute-start = (f32[16,120,128]{2,1,0:T(8,128)S(1)}, f32[16,120,128]{2,1,0:T(8,128)S(1)}, u32[]{:S(2)}, u32[]{:S(2)}) collective-permute-start(f32[16,120,128]{2,1,0:T(8,128)S(1)} %get-tuple-element.7), channel_id=1, source_target_pairs={{0,16},{16,0},{1,17},{17,1},{2,18},{18,2},{3,19},{19,3},{4,20},{20... | collective-permute-start | bytes 2949128 | tf_op jit(solution)/shard_map/ppermute | solution.py:285
  69.1 5.5 %collective-permute-start.1 = (f32[384,128]{1,0:T(8,128)}, f32[384,128]{1,0:T(8,128)}, u32[]{:S(2)}, u32[]{:S(2)}) collective-permute-start(f32[384,128]{1,0:T(8,128)} %bitcast.refs_0_), channel_id=1, source_target_pairs={{0,16},{16,0},{1,17},{17,1},{2,18},{18,2},{3,19},{19,3},{4,20},{20... | collective-permute-start | bytes 589832 | tf_op jit(solution)/shard_map/ppermute | solution.py:290

commit v2 on v1

v2 whole, which is shorter than its diff:
```python
import jax
import jax.numpy as jnp
from jax import lax
from jax.experimental import pallas as pl
from jax.experimental.pallas import tpu as pltpu
from jax.sharding import Mesh, PartitionSpec as P

F32 = jnp.float32
BF16 = jnp.bfloat16
ROWS = ("y", "zl", "core", "zh", "x")
PLANE = ("y", "x")
COLUMN = ("zl", "zh")
VMEM = pl.BlockSpec(memory_space=pltpu.VMEM)
ANY = pl.BlockSpec(memory_space=pl.ANY)
HBM = pl.BlockSpec(memory_space=pltpu.HBM)
PRODUCTS_VMEM = 50 << 20
SUMS_VMEM = 8 << 20
BASIS_VMEM = 32 << 20
CONTRACT0 = (((0,), (0,)), ((), ()))
BLOCKS = ((0, 0), (0, 1), (0, 2), (1, 1), (1, 2), (2, 2))


def split(value, parts):
    pieces = []
    for _ in range(parts):
        piece = value.astype(BF16)
        pieces.append(piece)
        value = value - piece.astype(F32)
    return pieces


def lanes(shape):
    return lax.broadcasted_iota(jnp.int32, shape, len(shape) - 1)


def products_kernel(x_hbm, c_hbm, r_hbm, mine_ref, other_ref, x_ref, c_ref, r_ref, g_acc, p_acc, sems):
    rows = x_ref.shape[0]
    cuts = ((0, rows // 3), (rows // 3, rows))
    loads = []
    for start, end in cuts:
        at = pl.ds(start, end - start)
        loads.append((x_hbm.at[at, :], x_ref.at[at, :]))
    loads.append((r_hbm, r_ref))
    for start, end in cuts:
        at = pl.ds(start, end - start)
        loads.append((c_hbm.at[at, :], c_ref.at[at, :]))
    loads = [pltpu.make_async_copy(src, dst, sems.at[i]) for i, (src, dst) in enumerate(loads)]
    for load in loads:
        load.start()

    s = None
    for load, (start, end) in zip(loads[:2], cuts):
        load.wait()
        x = x_ref[start:end, :]
        part = lax.dot_general(x, x, CONTRACT0, preferred_element_type=F32)
        s = part if s is None else s + part
    loads[2].wait()
    r = r_ref[...]
    t = sum(jnp.dot(p, r, preferred_element_type=F32) for p in split(s, 3))
    pieces = split(t, 3)
    at = 0
    for i in range(3):
        left = r[:, i * 128 : (i + 1) * 128]
        row = sum(
            lax.dot_general(left, p[:, i * 128 :], CONTRACT0, preferred_element_type=F32)
            for p in pieces
        )
        for j in range(3 - i):
            g_acc[at * 128 : (at + 1) * 128, :] = row[:, j * 128 : (j + 1) * 128]
            at += 1
    k = None
    for load, (start, end) in zip(loads[3:], cuts):
        load.wait()
        part = lax.dot_general(
            c_ref[start:end, :], x_ref[start:end, :], CONTRACT0, preferred_element_type=F32
        )
        k = part if k is None else k + part
    quarter = lanes((768, 128)) // 32
    turned = [k[:, :128]]
    for zh in range(1, 4):
        turned.append(pltpu.roll(k[:, zh * 128 : (zh + 1) * 128], zh * 32, 1))
    for n in range(4):
        out = turned[0]
        for zh in range(1, 4):
            out = jnp.where(quarter == (n + zh) % 4, turned[zh], out)
        p_acc[n] = out
    core = lax.axis_index("core")
    for side, ref in ((1 - core, other_ref), (core, mine_ref)):
        for y in range(4):
            for n in range(4):
                peer = y * 4 + n
                ref[peer, 0:24, :] = g_acc[pl.ds(pl.multiple_of(side * 384 + peer * 24, 8), 24), :]
                for zl in range(2):
                    start = pl.multiple_of((y * 4 + zl * 2 + side) * 48, 8)
                    ref[peer, 24 + zl * 48 : 72 + zl * 48, :] = p_acc[n, pl.ds(start, 48), :]


def products(x, c, r):
    half = jax.ShapeDtypeStruct((16, 120, 128), F32)
    return pl.pallas_call(
        products_kernel,
        in_specs=[HBM, HBM, HBM],
        out_specs=(VMEM, VMEM),
        out_shape=(half, half),
        scratch_shapes=[
            pltpu.VMEM(x.shape, BF16),
            pltpu.VMEM(c.shape, BF16),
            pltpu.VMEM(r.shape, BF16),
            pltpu.VMEM((768, 128), F32),
            pltpu.VMEM((4, 768, 128), F32),
            pltpu.SemaphoreType.DMA((5,)),
        ],
        compiler_params=pltpu.CompilerParams(vmem_limit_bytes=PRODUCTS_VMEM),
    )(x, c, r)


def column_kernel(got_ref, out_ref):
    total = got_ref[0]
    for i in range(1, 16):
        total = total + got_ref[i]
    gram = total[0:24]
    shares = pltpu.roll(total[24:120], (4 - lax.axis_index("x")) % 4 * 32, 1)
    lane = lanes((16, 128)) // 32
    for zl in range(2):
        for zh in range(4):
            peer = zl * 4 + zh
            out_ref[peer, 0:24, :] = gram
            out = jnp.zeros((16, 128), F32)
            for q in range(3):
                start = zl * 48 + q * 16
                piece = shares[start : start + 16]
                shift = ((q - zh) * 32) % 128
                if shift:
                    piece = pltpu.roll(piece, shift, 1)
                out = jnp.where(lane == q, piece, out)
            out_ref[peer, 24:40, :] = out


def column_blocks(got):
    return pl.pallas_call(
        column_kernel,
        in_specs=[VMEM],
        out_specs=VMEM,
        out_shape=jax.ShapeDtypeStruct((8, 40, 128), F32),
        compiler_params=pltpu.CompilerParams(vmem_limit_bytes=SUMS_VMEM),
    )(got)


def plane_kernel(got_ref, gram_ref, cosketch_ref):
    total = got_ref[0]
    for i in range(1, 8):
        total = total + got_ref[i]
    for i in range(16):
        gram_ref[i] = total[0:24]
    share = total[24:40]
    rows = [share, pltpu.roll(share, 96, 1), pltpu.roll(share, 64, 1)]
    cosketch_ref[...] = jnp.concatenate(rows, axis=0).T[0:32, :]


def plane_blocks(got):
    return pl.pallas_call(
        plane_kernel,
        in_specs=[VMEM],
        out_specs=(VMEM, VMEM),
        out_shape=(
            jax.ShapeDtypeStruct((16, 24, 128), F32),
            jax.ShapeDtypeStruct((32, 48), F32),
        ),
        compiler_params=pltpu.CompilerParams(vmem_limit_bytes=SUMS_VMEM),
    )(got)


def spread(value):
    return jnp.broadcast_to(value, (8, 128))


def inverse_factor(block, same, beside=None):
    n, half = 16, 8
    d = [block[8 * i : 8 * i + 8, :] for i in range(n)]
    row = lax.broadcasted_iota(jnp.int32, (8, 128), 0)
    lane = lanes((8, 128))
    v = [jnp.where(lane == row + 8 * i, 1.0, 0.0).astype(F32) for i in range(n)]

    def stacked(rows):
        out = rows[0]
        for j in range(1, 8):
            out = jnp.where(row == j, rows[j], out)
        return out

    def columns_of(k, p):
        return [spread(d[k][:, 8 * p + j : 8 * p + j + 1]) for j in range(8)]

    def reader(values, at):
        for j, value in enumerate(values):
            same[at + 8 * j : at + 8 * j + 8, :] = value
        return lambda j, k: same[pl.ds(at + 8 * j + k, 8, stride=0), :]

    def rows_of(value, at):
        read = reader([value], at)
        return [read(0, j) for j in range(8)]

    own, u = columns_of(0, 0), []
    for p in range(n):
        base = (p % 2) * 160
        read = reader(own, base)
        s = [[read(j, k) if k >= j else None for j in range(8)] for k in range(8)]
        last = p == n - 1
        ahead = not last and p != half - 1
        if ahead:
            below, own = columns_of(p + 1, p), columns_of(p + 1, p + 1)
        r = []
        for j in range(8):
            r.append(lax.rsqrt(s[j][j]))
            for k in range(j + 1, 8):
                s[k][j] = s[k][j] * r[j]
            for m in range(j + 1, 8):
                for k in range(m, 8):
                    s[k][m] = s[k][m] - s[k][j] * s[m][j]

        def forward(rows):
            done = []
            for j in range(8):
                value = rows[j]
                for i in range(j):
                    value = value - s[j][i] * done[i]
                done.append(value * r[j])
            return done

        if ahead:
            below = forward(below)
            read = reader(below, base + 64)
            for m in range(8):
                for j in range(8):
                    own[m] = own[m] - below[j] * read(j, m)
        vx = forward(rows_of(v[p], base + 128))
        v[p] = stacked(vx)
        if not last:
            dx = forward(rows_of(d[p], base + 136))
            u.append(stacked(dx))
        if beside is not None:
            beside(p)
        for k in range(p + 1, half if p < half else n):
            factors = below if k == p + 1 else forward(columns_of(k, p))
            for j in range(8):
                d[k] = d[k] - factors[j] * dx[j]
                v[k] = v[k] - factors[j] * vx[j]
        if p == half - 1:
            top = jnp.concatenate(u, axis=0)
            both = jnp.where(lanes((64, 128)) < 64, jnp.concatenate(v[:half], axis=0), top)
            minus = exact(top, both, CONTRACT0)
            for k in range(half, n):
                part = minus[8 * k : 8 * k + 8]
                d[k] = d[k] - part
                v[k] = jnp.where(lane < 64, -part, v[k])
            own = columns_of(half, half)
    return jnp.concatenate(v, axis=0)


def exact(a, b, contract=(((1,), (0,)), ((), ()))):
    return lax.dot_general(a, b, contract, precision=lax.Precision.HIGHEST, preferred_element_type=F32)


def basis_kernel(scale, a_ref, b_ref, r_ref, x_hbm, out_hbm, g, x_vmem, out_vmem, same, in_sem, out_sem):
    load = pltpu.make_async_copy(x_hbm, x_vmem, in_sem)
    load.start()
    core = lax.axis_index("core")
    g[pl.ds(pl.multiple_of(core * 384, 8), 384), :] = a_ref[...]
    g[pl.ds(pl.multiple_of((1 - core) * 384, 8), 384), :] = b_ref[...]
    rows = x_vmem.shape[0]
    stores = []

    def block(i):
        return g[i * 128 : (i + 1) * 128, :]

    def columns(i, inverse, pieces, copies):
        left = r_ref[:, : inverse.shape[1]]
        weight = sum(
            lax.dot_general(left, p, (((1,), (1,)), ((), ())), preferred_element_type=F32)
            for p in split(inverse, 3)
        )
        weight = jnp.concatenate(split(weight * scale, 2), axis=1)
        size, every = rows // pieces, pieces // copies

        def piece(p):
            at = pl.ds(p * size, size)
            both = jnp.dot(x_vmem[at, :], weight, preferred_element_type=F32)
            out_vmem[i, at, :] = both[:, :128] + both[:, 128:]
            if p % every == every - 1:
                at = pl.ds((p + 1 - every) * size, every * size)
                store = pltpu.make_async_copy(
                    out_vmem.at[i, at, :],
                    out_hbm.at[at, pl.ds(i * 128, 128)],
                    out_sem.at[len(stores)],
                )
                store.start()
                stores.append(store)

        return piece

    m0 = inverse_factor(block(0), same)
    row0 = exact(m0, jnp.concatenate([block(1), block(2)], axis=1))
    minus = exact(row0, row0, CONTRACT0)
    left = -exact(row0, m0, CONTRACT0)
    load.wait()
    m1 = inverse_factor(block(3) - minus[:128, :128], same, columns(0, m0, 16, 2))
    row1 = exact(m1, block(4) - minus[:128, 128:])
    last = block(5) - minus[128:, 128:] - exact(row1, row1, CONTRACT0)
    v1 = jnp.concatenate([exact(m1, left[:128]), m1], axis=1)
    below = jnp.concatenate([left[128:], jnp.zeros((128, 128), F32)], axis=1) - exact(row1, v1, CONTRACT0)
    m2 = inverse_factor(last, same, columns(1, v1, 16, 2))
    piece = columns(2, jnp.concatenate([exact(m2, below), m2], axis=1), 4, 4)
    for p in range(4):
        piece(p)
    for store in stores:
        store.wait()


def basis_of(scale, a, b, r, x):
    return pl.pallas_call(
        lambda *refs: basis_kernel(scale, *refs),
        in_specs=[VMEM, VMEM, VMEM, ANY],
        out_specs=ANY,
        out_shape=jax.ShapeDtypeStruct((x.shape[0], 384), F32),
        scratch_shapes=[
            pltpu.VMEM((768, 128), F32),
            pltpu.VMEM(x.shape, BF16),
            pltpu.VMEM((3, x.shape[0], 128), F32),
            pltpu.VMEM((320, 128), F32),
            pltpu.SemaphoreType.DMA,
            pltpu.SemaphoreType.DMA((8,)),
        ],
        compiler_params=pltpu.CompilerParams(vmem_limit_bytes=BASIS_VMEM),
    )(a, b, r, x)


def per_device(snapshots, range_test, corange_test):
    total = snapshots.shape[0] * 256
    swap = [(0, 1), (1, 0)]
    mine, other = products(snapshots, corange_test, range_test)
    pair = mine + lax.ppermute(other, "core", swap)
    got = lax.all_to_all(pair, PLANE, 0, 0, tiled=True)
    got = lax.all_to_all(column_blocks(got), COLUMN, 0, 0, tiled=True)
    gram, cosketch = plane_blocks(got)
    half = lax.all_to_all(gram, PLANE, 0, 0, tiled=True).reshape(384, 128)
    basis = basis_of(float(total) ** 0.5, half, lax.ppermute(half, "core", swap), range_test, snapshots)
    return basis, cosketch.T


def solution(mesh):
    fine = Mesh(mesh.devices.reshape(4, 2, 2, 4, 4), ROWS)
    in_specs = (P(ROWS, None), P(), P(ROWS, None))
    out_specs = (P(ROWS, None), P(("y", "zl", "core"), ("zh", "x")))
    return jax.shard_map(
        per_device, mesh=fine, in_specs=in_specs, out_specs=out_specs, check_vma=False
    )
```

time: 97.6 us -> 80.2 us (0.82)
  Pallas kernels: 34.9 us -> 21.6 us
  local copies, waits for them, and re-layouts: 4.31 us -> 1 us
  blocking collectives: 47.4 us -> 46 us
  waiting for transfers between devices: 2.2 us -> 3.26 us
    pallas_call x2, Pallas kernels: 31.3 us -> 20.7 us  [the longest x1 12.2 us: basis_of(): pl.pallas_call(lambda *refs: basis_kernel(scale, *refs), in_specs=[VMEM,...]
    unnamed x9 -> x4, local copies, waits for them, and re-layouts: 4.31 us -> 1 us
    pallas_call x1, Pallas kernels: 1.99 us -> 0.19 us  [column_blocks(): pl.pallas_call(column_kernel, in_specs=[VMEM], out_specs=VMEM, out_shape=...]
    ppermute x1, waiting for transfers between devices: 0.01 us -> 1.07 us  [per_device(): lax.ppermute(half, 'core', swap)]
  transfers between devices with their start and end apart: 2 -> 2, of which waited for: 1 -> 2; matrix products, arithmetic and copies ran while one was open for 1% -> 0% of each run, Pallas kernels for 0% -> 0%
where the time goes in v2:
time: 80.2 us; the launch traced here: 79.9 us
  blocking collectives  46 us (57%)
  Pallas kernels  21.6 us (27%)
  starting transfers between devices  7.11 us (9%)
  waiting for transfers between devices  3.26 us (4%)
  local copies, waits for them, and re-layouts  1 us (1%)
  between operations  0.83 us (1%)
    all_to_all x1, blocking collectives, per_device(): got = lax.all_to_all(pair, PLANE, 0, 0, tiled=True)  20.4 us
    all_to_all x1, blocking collectives, per_device(): got = lax.all_to_all(column_blocks(got), COLUMN, 0, 0, tiled=True)  15.1 us
    pallas_call x1, Pallas kernels, basis_of(): pl.pallas_call(lambda *refs: basis_kernel(scale, *refs), in_specs=[VMEM,...  12.2 us
    all_to_all x1, blocking collectives, per_device(): half = lax.all_to_all(gram, PLANE, 0, 0, tiled=True).reshape(384, 128)  10.5 us
    pallas_call x1, Pallas kernels, products(): pl.pallas_call(products_kernel, in_specs=[HBM, HBM, HBM], out_specs=(VMEM...  8.44 us
    ppermute x1, starting transfers between devices, per_device(): lax.ppermute(half, 'core', swap)  3.8 us
    ppermute x1, starting transfers between devices, per_device(): pair = mine + lax.ppermute(other, 'core', swap)  3.31 us
    ppermute x1, waiting for transfers between devices, per_device(): pair = mine + lax.ppermute(other, 'core', swap)  2.19 us
  transfers between devices with their start and end apart: 2, of which 2 were waited for; matrix products, arithmetic and copies ran while one was open for 0% of the time, Pallas kernels for 0%

profile of v2, /device:TPU:1, one launch (start us, length us, event | category | flops | bytes accessed | tf_op | source)
XLA Modules:
  0.0 79.9 jit_solution(4390615330237613170)
XLA Ops:
  0.6 0.0 copy-start.1
  0.6 1.0 %copy-done.1 = bf16[512,384]{1,0:T(8,128)(2,1)S(1)} copy-done((bf16[512,384]{1,0:T(8,128)(2,1)S(1)}, bf16[512,384]{1,0:T(8,128)(2,1)}, u32[]{:S(2)}) %copy-start.1) | copy-done | bytes 393240
  1.6 8.4 %shard_map.50 = (f32[16,120,128]{2,1,0:T(8,128)S(1)}, f32[16,120,128]{2,1,0:T(8,128)S(1)}) custom-call(bf16[3072,512]{1,0:T(8,128)(2,1)} %refs_3_.1, bf16[3072,768]{1,0:T(8,128)(2,1)} %c_hbm.1, bf16[512,384]{1,0:T(8,128)(2,1)S(1)} %copy-done.1), custom_call_target="tpu_custom_call" | custom-call | tf_op jit(solution)/shard_map/pallas_call | solution.py:100
  10.1 0.0 copy-start
  10.1 3.3 %collective-permute-start = (f32[16,120,128]{2,1,0:T(8,128)S(1)}, f32[16,120,128]{2,1,0:T(8,128)S(1)}, u32[]{:S(2)}, u32[]{:S(2)}) collective-permute-start(f32[16,120,128]{2,1,0:T(8,128)S(1)} %get-tuple-element.7), channel_id=1, source_target_pairs={{0,16},{16,0},{1,17},{17,1},{2,18},{18,2},{3,19},{19,3},{4,20},{20... | collective-permute-start | bytes 2949128 | tf_op jit(solution)/shard_map/ppermute | solution.py:340
  13.4 2.2 %collective-permute-done = f32[16,120,128]{2,1,0:T(8,128)S(1)} collective-permute-done((f32[16,120,128]{2,1,0:T(8,128)S(1)}, f32[16,120,128]{2,1,0:T(8,128)S(1)}, u32[]{:S(2)}, u32[]{:S(2)}) %collective-permute-start) | collective-permute-done | bytes 983072 | tf_op jit(solution)/shard_map/ppermute | solution.py:340
  15.6 0.1 add.3
  15.7 20.4 %all_to_all.15.got_ref = f32[16,120,128]{2,1,0:T(8,128)S(1)} all-to-all(f32[16,120,128]{2,1,0:T(8,128)S(1)} %add.3), channel_id=1, replica_groups=mesh['y'=4,'zl'=2,'core'=2,'zh'=4,'x'=4] {'y','x'}, dimensions={0} | all-to-all | bytes 1966080 | tf_op jit(solution)/shard_map/all_to_all | solution.py:341
  36.1 0.2 shard_map.51
  36.3 15.1 %all_to_all.16.got_ref = f32[8,40,128]{2,1,0:T(8,128)S(1)} all-to-all(f32[8,40,128]{2,1,0:T(8,128)S(1)} %shard_map.51), channel_id=1, replica_groups=mesh['y'=4,'zl'=2,'core'=2,'zh'=4,'x'=4] {'zl','zh'}, dimensions={0} | all-to-all | bytes 327680 | tf_op jit(solution)/shard_map/all_to_all | solution.py:342
  51.5 0.8 shard_map.52
  52.2 10.5 %all_to_all.17 = f32[16,24,128]{2,1,0:T(8,128)S(1)} all-to-all(f32[16,24,128]{2,1,0:T(8,128)S(1)} %get-tuple-element.8), channel_id=1, replica_groups=mesh['y'=4,'zl'=2,'core'=2,'zh'=4,'x'=4] {'y','x'}, dimensions={0} | all-to-all | bytes 393216 | tf_op jit(solution)/shard_map/all_to_all | solution.py:344
  62.7 3.8 %collective-permute-start.1 = (f32[384,128]{1,0:T(8,128)S(1)}, f32[384,128]{1,0:T(8,128)S(1)}, u32[]{:S(2)}, u32[]{:S(2)}) collective-permute-start(f32[384,128]{1,0:T(8,128)S(1)} %bitcast.2), channel_id=1, source_target_pairs={{0,16},{16,0},{1,17},{17,1},{2,18},{18,2},{3,19},{19,3},{4,20},{20... | collective-permute-start | bytes 589832 | tf_op jit(solution)/shard_map/ppermute | solution.py:345
  66.5 1.1 %collective-permute-done.1.refs_1_ = f32[384,128]{1,0:T(8,128)S(1)} collective-permute-done((f32[384,128]{1,0:T(8,128)S(1)}, f32[384,128]{1,0:T(8,128)S(1)}, u32[]{:S(2)}, u32[]{:S(2)}) %collective-permute-start.1) | collective-permute-done | bytes 196640 | tf_op jit(solution)/shard_map/ppermute | solution.py:345
  67.5 0.0 copy-done
  67.5 12.2 %shard_map.53 = f32[3072,384]{1,0:T(8,128)} custom-call(f32[384,128]{1,0:T(8,128)S(1)} %bitcast.3, f32[384,128]{1,0:T(8,128)S(1)} %collective-permute-done.1.refs_1_, bf16[512,384]{1,0:T(8,128)(2,1)S(1)} %copy-done.1, bf16[3072,512]{1,0:T(8,128)(2,1)S(1)} %copy-done), custom_call_target="tpu_custom_call" | custom-call | tf_op jit(solution)/shard_map/pallas_call | solution.py:319
Async XLA Ops:
  0.6 1.0 %copy-start.1 = (bf16[512,384]{1,0:T(8,128)(2,1)S(1)}, bf16[512,384]{1,0:T(8,128)(2,1)}, u32[]{:S(2)}) copy-start(bf16[512,384]{1,0:T(8,128)(2,1)} %refs_2_.1) | copy-start | bytes 1179652
  10.1 57.5 %copy-start = (bf16[3072,512]{1,0:T(8,128)(2,1)S(1)}, bf16[3072,512]{1,0:T(8,128)(2,1)}, u32[]{:S(2)}) copy-start(bf16[3072,512]{1,0:T(8,128)(2,1)} %refs_3_.1) | copy-start | bytes 9437188
  10.1 5.5 %collective-permute-start = (f32[16,120,128]{2,1,0:T(8,128)S(1)}, f32[16,120,128]{2,1,0:T(8,128)S(1)}, u32[]{:S(2)}, u32[]{:S(2)}) collective-permute-start(f32[16,120,128]{2,1,0:T(8,128)S(1)} %get-tuple-element.7), channel_id=1, source_target_pairs={{0,16},{16,0},{1,17},{17,1},{2,18},{18,2},{3,19},{19,3},{4,20},{20... | collective-permute-start | bytes 2949128 | tf_op jit(solution)/shard_map/ppermute | solution.py:340
  62.7 4.9 %collective-permute-start.1 = (f32[384,128]{1,0:T(8,128)S(1)}, f32[384,128]{1,0:T(8,128)S(1)}, u32[]{:S(2)}, u32[]{:S(2)}) collective-permute-start(f32[384,128]{1,0:T(8,128)S(1)} %bitcast.2), channel_id=1, source_target_pairs={{0,16},{16,0},{1,17},{17,1},{2,18},{18,2},{3,19},{19,3},{4,20},{20... | collective-permute-start | bytes 589832 | tf_op jit(solution)/shard_map/ppermute | solution.py:345

commit v3 on v2

--- a/solution.py
+++ b/solution.py
@@ -12,8 +12,9 @@
 COLUMN = ("zl", "zh")
 VMEM = pl.BlockSpec(memory_space=pltpu.VMEM)
 ANY = pl.BlockSpec(memory_space=pl.ANY)
-HBM = pl.BlockSpec(memory_space=pltpu.HBM)
-PRODUCTS_VMEM = 50 << 20
+CORANGE_VMEM = 48 << 20
+CORANGE_PARTS = 6
+GRAM_VMEM = 32 << 20
 SUMS_VMEM = 8 << 20
 BASIS_VMEM = 32 << 20
 CONTRACT0 = (((0,), (0,)), ((), ()))
@@ -33,47 +34,28 @@
     return lax.broadcasted_iota(jnp.int32, shape, len(shape) - 1)
 
 
-def products_kernel(x_hbm, c_hbm, r_hbm, mine_ref, other_ref, x_ref, c_ref, r_ref, g_acc, p_acc, sems):
-    rows = x_ref.shape[0]
-    cuts = ((0, rows // 3), (rows // 3, rows))
-    loads = []
-    for start, end in cuts:
-        at = pl.ds(start, end - start)
-        loads.append((x_hbm.at[at, :], x_ref.at[at, :]))
-    loads.append((r_hbm, r_ref))
-    for start, end in cuts:
-        at = pl.ds(start, end - start)
-        loads.append((c_hbm.at[at, :], c_ref.at[at, :]))
-    loads = [pltpu.make_async_copy(src, dst, sems.at[i]) for i, (src, dst) in enumerate(loads)]
+def loads_of(pairs, sems):
+    loads = [pltpu.make_async_copy(src, dst, sems.at[i]) for i, (src, dst) in enumerate(pairs)]
     for load in loads:
         load.start()
-
-    s = None
-    for load, (start, end) in zip(loads[:2], cuts):
-        load.wait()
-        x = x_ref[start:end, :]
-        part = lax.dot_general(x, x, CONTRACT0, preferred_element_type=F32)
-        s = part if s is None else s + part
-    loads[2].wait()
-    r = r_ref[...]
-    t = sum(jnp.dot(p, r, preferred_element_type=F32) for p in split(s, 3))
-    pieces = split(t, 3)
-    at = 0
-    for i in range(3):
-        left = r[:, i * 128 : (i + 1) * 128]
-        row = sum(
-            lax.dot_general(left, p[:, i * 128 :], CONTRACT0, preferred_element_type=F32)
-            for p in pieces
-        )
-        for j in range(3 - i):
-            g_acc[at * 128 : (at + 1) * 128, :] = row[:, j * 128 : (j + 1) * 128]
-            at += 1
+    return loads
+
+
+def cuts_of(rows, parts):
+    return [pl.ds(i * rows // parts, rows // parts) for i in range(parts)]
+
+
+def corange_kernel(x_hbm, c_hbm, mine_ref, other_ref, x_ref, c_ref, p_acc, sems):
+    cuts = cuts_of(x_ref.shape[0], CORANGE_PARTS)
+    pairs = []
+    for at in cuts:
+        pairs += [(x_hbm.at[at, :], x_ref.at[at, :]), (c_hbm.at[at, :], c_ref.at[at, :])]
+    loads = loads_of(pairs, sems)
     k = None
-    for load, (start, end) in zip(loads[3:], cuts):
-        load.wait()
-        part = lax.dot_general(
-            c_ref[start:end, :], x_ref[start:end, :], CONTRACT0, preferred_element_type=F32
-        )
+    for i, at in enumerate(cuts):
+        loads[2 * i].wait()
+        loads[2 * i + 1].wait()
+        part = lax.dot_general(c_ref[at, :], x_ref[at, :], CONTRACT0, preferred_element_type=F32)
         k = part if k is None else k + part
     quarter = lanes((768, 128)) // 32
     turned = [k[:, :128]]
@@ -88,30 +70,75 @@
     for side, ref in ((1 - core, other_ref), (core, mine_ref)):
         for y in range(4):
             for n in range(4):
-                peer = y * 4 + n
-                ref[peer, 0:24, :] = g_acc[pl.ds(pl.multiple_of(side * 384 + peer * 24, 8), 24), :]
                 for zl in range(2):
                     start = pl.multiple_of((y * 4 + zl * 2 + side) * 48, 8)
-                    ref[peer, 24 + zl * 48 : 72 + zl * 48, :] = p_acc[n, pl.ds(start, 48), :]
-
-
-def products(x, c, r):
-    half = jax.ShapeDtypeStruct((16, 120, 128), F32)
-    return pl.pallas_call(
-        products_kernel,
-        in_specs=[HBM, HBM, HBM],
+                    ref[y * 4 + n, zl * 48 : 48 + zl * 48, :] = p_acc[n, pl.ds(start, 48), :]
+
+
+def corange_of(x, c):
+    half = jax.ShapeDtypeStruct((16, 96, 128), F32)
+    return pl.pallas_call(
+        corange_kernel,
+        in_specs=[ANY, ANY],
+        out_specs=(VMEM, VMEM, VMEM),
+        out_shape=(half, half, jax.ShapeDtypeStruct(x.shape, BF16)),
+        scratch_shapes=[
+            pltpu.VMEM(c.shape, BF16),
+            pltpu.VMEM((4, 768, 128), F32),
+            pltpu.SemaphoreType.DMA((2 * CORANGE_PARTS,)),
+        ],
+        compiler_params=pltpu.CompilerParams(vmem_limit_bytes=CORANGE_VMEM),
+    )(x, c)
+
+
+def gram_kernel(x_ref, r_ref, mine_ref, other_ref, g_acc):
+    x = x_ref[...]
+    s = lax.dot_general(x, x, CONTRACT0, preferred_element_type=F32)
+    r = r_ref[...]
+    t = sum(jnp.dot(p, r, preferred_element_type=F32) for p in split(s, 3))
+    pieces = split(t, 3)
+    at = 0
+    for i in range(3):
+        left = r[:, i * 128 : (i + 1) * 128]
+        row = sum(
+            lax.dot_general(left, p[:, i * 128 :], CONTRACT0, preferred_element_type=F32)
+            for p in pieces
+        )
+        for j in range(3 - i):
+            g_acc[at * 128 : (at + 1) * 128, :] = row[:, j * 128 : (j + 1) * 128]
+            at += 1
+    core = lax.axis_index("core")
+    mine_ref[...] = g_acc[pl.ds(pl.multiple_of(core * 384, 8), 384), :]
+    other_ref[...] = g_acc[pl.ds(pl.multiple_of((1 - core) * 384, 8), 384), :]
+
+
+def gram_of(x, r):
+    half = jax.ShapeDtypeStruct((384, 128), F32)
+    return pl.pallas_call(
+        gram_kernel,
+        in_specs=[VMEM, VMEM],
         out_specs=(VMEM, VMEM),
         out_shape=(half, half),
-        scratch_shapes=[
-            pltpu.VMEM(x.shape, BF16),
-            pltpu.VMEM(c.shape, BF16),
-            pltpu.VMEM(r.shape, BF16),
-            pltpu.VMEM((768, 128), F32),
-            pltpu.VMEM((4, 768, 128), F32),
-            pltpu.SemaphoreType.DMA((5,)),
-        ],
-        compiler_params=pltpu.CompilerParams(vmem_limit_bytes=PRODUCTS_VMEM),
-    )(x, c, r)
+        scratch_shapes=[pltpu.VMEM((768, 128), F32)],
+        compiler_params=pltpu.CompilerParams(vmem_limit_bytes=GRAM_VMEM),
+    )(x, r)
+
+
+def pair_kernel(gram_ref, gram_got, share_ref, share_got, out_ref):
+    for peer in range(16):
+        at = pl.ds(peer * 24, 24)
+        out_ref[peer, 0:24, :] = gram_ref[at, :] + gram_got[at, :]
+        out_ref[peer, 24:120, :] = share_ref[peer] + share_got[peer]
+
+
+def pair_blocks(*args):
+    return pl.pallas_call(
+        pair_kernel,
+        in_specs=[VMEM] * 4,
+        out_specs=VMEM,
+        out_shape=jax.ShapeDtypeStruct((16, 120, 128), F32),
+        compiler_params=pltpu.CompilerParams(vmem_limit_bytes=SUMS_VMEM),
+    )(*args)
 
 
 def column_kernel(got_ref, out_ref):
@@ -146,15 +173,13 @@
     )(got)
 
 
-def plane_kernel(got_ref, gram_ref, cosketch_ref):
+def plane_kernel(got_ref, gram_ref, share_ref):
     total = got_ref[0]
     for i in range(1, 8):
         total = total + got_ref[i]
     for i in range(16):
         gram_ref[i] = total[0:24]
-    share = total[24:40]
-    rows = [share, pltpu.roll(share, 96, 1), pltpu.roll(share, 64, 1)]
-    cosketch_ref[...] = jnp.concatenate(rows, axis=0).T[0:32, :]
+    share_ref[...] = total[24:40]
 
 
 def plane_blocks(got):
@@ -164,7 +189,7 @@
         out_specs=(VMEM, VMEM),
         out_shape=(
             jax.ShapeDtypeStruct((16, 24, 128), F32),
-            jax.ShapeDtypeStruct((32, 48), F32),
+            jax.ShapeDtypeStruct((16, 128), F32),
         ),
         compiler_params=pltpu.CompilerParams(vmem_limit_bytes=SUMS_VMEM),
     )(got)
@@ -260,89 +285,119 @@
     return lax.dot_general(a, b, contract, precision=lax.Precision.HIGHEST, preferred_element_type=F32)
 
 
-def basis_kernel(scale, a_ref, b_ref, r_ref, x_hbm, out_hbm, g, x_vmem, out_vmem, same, in_sem, out_sem):
-    load = pltpu.make_async_copy(x_hbm, x_vmem, in_sem)
-    load.start()
+def basis_kernel(scale, a_ref, b_ref, share_ref, r_ref, x_ref, out_hbm, cosketch_ref, g, out_vmem, y_ref, same, out_sem):
     core = lax.axis_index("core")
     g[pl.ds(pl.multiple_of(core * 384, 8), 384), :] = a_ref[...]
     g[pl.ds(pl.multiple_of((1 - core) * 384, 8), 384), :] = b_ref[...]
-    rows = x_vmem.shape[0]
+    rows = x_ref.shape[0]
     stores = []
 
     def block(i):
         return g[i * 128 : (i + 1) * 128, :]
 
-    def columns(i, inverse, pieces, copies):
+    def weight_of(inverse):
         left = r_ref[:, : inverse.shape[1]]
         weight = sum(
             lax.dot_general(left, p, (((1,), (1,)), ((), ())), preferred_element_type=F32)
             for p in split(inverse, 3)
         )
-        weight = jnp.concatenate(split(weight * scale, 2), axis=1)
+        return jnp.concatenate(split(weight, 2), axis=1)
+
+    def times(left, weight):
+        both = jnp.dot(left, weight, preferred_element_type=F32)
+        return both[:, :128] + both[:, 128:]
+
+    def columns(i, inverse, pieces, copies):
+        weight = weight_of(inverse * scale)
         size, every = rows // pieces, pieces // copies
 
         def piece(p):
             at = pl.ds(p * size, size)
-            both = jnp.dot(x_vmem[at, :], weight, preferred_element_type=F32)
-            out_vmem[i, at, :] = both[:, :128] + both[:, 128:]
+            out_vmem[i, at, :] = times(x_ref[at, :], weight)
             if p % every == every - 1:
-                at = pl.ds((p + 1 - every) * size, every * size)
-                store = pltpu.make_async_copy(
-                    out_vmem.at[i, at, :],
-                    out_hbm.at[at, pl.ds(i * 128, 128)],
-                    out_sem.at[len(stores)],
-                )
-                store.start()
-                stores.append(store)
+                store(i, (p + 1 - every) * size, every * size)
 
         return piece
 
+    def store(i, start, size):
+        at = pl.ds(start, size)
+        stores.append(
+            pltpu.make_async_copy(
+                out_vmem.at[i, at, :], out_hbm.at[at, pl.ds(i * 128, 128)], out_sem.at[len(stores)]
+            )
+        )
+        stores[-1].start()
+
+    share = share_ref[...]
+    turned = [share, pltpu.roll(share, 96, 1), pltpu.roll(share, 64, 1)]
+    cosketch_ref[...] = jnp.concatenate(turned, axis=0).T[0:32, :]
     m0 = inverse_factor(block(0), same)
     row0 = exact(m0, jnp.concatenate([block(1), block(2)], axis=1))
     minus = exact(row0, row0, CONTRACT0)
     left = -exact(row0, m0, CONTRACT0)
-    load.wait()
     m1 = inverse_factor(block(3) - minus[:128, :128], same, columns(0, m0, 16, 2))
     row1 = exact(m1, block(4) - minus[:128, 128:])
     last = block(5) - minus[128:, 128:] - exact(row1, row1, CONTRACT0)
     v1 = jnp.concatenate([exact(m1, left[:128]), m1], axis=1)
     below = jnp.concatenate([left[128:], jnp.zeros((128, 128), F32)], axis=1) - exact(row1, v1, CONTRACT0)
-    m2 = inverse_factor(last, same, columns(1, v1, 16, 2))
-    piece = columns(2, jnp.concatenate([exact(m2, below), m2], axis=1), 4, 4)
+    one = jnp.where(lanes((128, 128)) == lax.broadcasted_iota(jnp.int32, (128, 128), 0), 1.0, 0.0)
+    first = columns(1, v1, 16, 2)
+    weight = weight_of(jnp.concatenate([below[:, :256], one.astype(F32)], axis=1))
+    size = rows // 16
+
+    def beside(p):
+        first(p)
+        at = pl.ds(p * size, size)
+        y_ref[at, :] = jnp.concatenate(split(times(x_ref[at, :], weight), 2), axis=1)
+
+    m2 = inverse_factor(last, same, beside)
+    high, low = split(m2.T * scale, 2)
+    weight = jnp.concatenate(
+        [jnp.concatenate([high, low], axis=1), jnp.concatenate([high, jnp.zeros_like(low)], axis=1)], axis=0
+    )
+    size = rows // 4
     for p in range(4):
-        piece(p)
-    for store in stores:
-        store.wait()
-
-
-def basis_of(scale, a, b, r, x):
+        at = pl.ds(p * size, size)
+        out_vmem[2, at, :] = times(y_ref[at, :], weight)
+        store(2, p * size, size)
+    for copy in stores:
+        copy.wait()
+
+
+def basis_of(scale, a, b, share, r, x):
     return pl.pallas_call(
         lambda *refs: basis_kernel(scale, *refs),
-        in_specs=[VMEM, VMEM, VMEM, ANY],
-        out_specs=ANY,
-        out_shape=jax.ShapeDtypeStruct((x.shape[0], 384), F32),
+        in_specs=[VMEM] * 5,
+        out_specs=(ANY, VMEM),
+        out_shape=(
+            jax.ShapeDtypeStruct((x.shape[0], 384), F32),
+            jax.ShapeDtypeStruct((32, 48), F32),
+        ),
         scratch_shapes=[
             pltpu.VMEM((768, 128), F32),
-            pltpu.VMEM(x.shape, BF16),
             pltpu.VMEM((3, x.shape[0], 128), F32),
+            pltpu.VMEM((x.shape[0], 256), BF16),
             pltpu.VMEM((320, 128), F32),
-            pltpu.SemaphoreType.DMA,
             pltpu.SemaphoreType.DMA((8,)),
         ],
         compiler_params=pltpu.CompilerParams(vmem_limit_bytes=BASIS_VMEM),
-    )(a, b, r, x)
+    )(a, b, share, r, x)
 
 
 def per_device(snapshots, range_test, corange_test):
     total = snapshots.shape[0] * 256
     swap = [(0, 1), (1, 0)]
-    mine, other = products(snapshots, corange_test, range_test)
-    pair = mine + lax.ppermute(other, "core", swap)
+    share, share_out, held = corange_of(snapshots, corange_test)
+    share_got = lax.ppermute(share_out, "core", swap)
+    gram, gram_out = gram_of(held, range_test)
+    gram_got = lax.ppermute(gram_out, "core", swap)
+    pair = pair_blocks(gram, gram_got, share, share_got)
     got = lax.all_to_all(pair, PLANE, 0, 0, tiled=True)
     got = lax.all_to_all(column_blocks(got), COLUMN, 0, 0, tiled=True)
-    gram, cosketch = plane_blocks(got)
+    gram, share = plane_blocks(got)
     half = lax.all_to_all(gram, PLANE, 0, 0, tiled=True).reshape(384, 128)
-    basis = basis_of(float(total) ** 0.5, half, lax.ppermute(half, "core", swap), range_test, snapshots)
+    other = lax.ppermute(half, "core", swap)
+    basis, cosketch = basis_of(float(total) ** 0.5, half, other, share, range_test, held)
     return basis, cosketch.T
 
 

time: 80.2 us -> 77.3 us (0.964)
  Pallas kernels: 21.6 us -> 20.5 us
  local copies, waits for them, and re-layouts: 1 us -> 0.01 us
    unnamed x4 -> x2, local copies, waits for them, and re-layouts: 1 us -> 0.01 us
    ppermute x2 -> x3, waiting for transfers between devices: 3.26 us -> 2.49 us  [the longest x1 1.41 us: per_device(): gram_got = lax.ppermute(gram_out, 'core', swap)]
    pallas_call x2 -> x4, Pallas kernels: 20.7 us -> 20.3 us  [the longest x1 11.8 us: basis_of(): pl.pallas_call(lambda *refs: basis_kernel(scale, *refs), in_specs=[VMEM]...]
    ppermute x2 -> x3, starting transfers between devices: 7.11 us -> 7.16 us  [the longest x1 3.76 us: per_device(): other = lax.ppermute(half, 'core', swap)]
  transfers between devices with their start and end apart: 2 -> 3, of which waited for: 2 -> 2; matrix products, arithmetic and copies ran while one was open for 0% -> 0% of each run, Pallas kernels for 0% -> 4%
where the time goes in v3:
time: 77.3 us; the launch traced here: 77.1 us
  blocking collectives  46.1 us (60%)
  Pallas kernels  20.5 us (27%)
  starting transfers between devices  7.16 us (9%)
  waiting for transfers between devices  2.49 us (3%)
  between operations  0.83 us (1%)
    all_to_all x1, blocking collectives, per_device(): got = lax.all_to_all(pair, PLANE, 0, 0, tiled=True)  20.7 us
    all_to_all x1, blocking collectives, per_device(): got = lax.all_to_all(column_blocks(got), COLUMN, 0, 0, tiled=True)  15.1 us
    pallas_call x1, Pallas kernels, basis_of(): pl.pallas_call(lambda *refs: basis_kernel(scale, *refs), in_specs=[VMEM]...  11.8 us
    all_to_all x1, blocking collectives, per_device(): half = lax.all_to_all(gram, PLANE, 0, 0, tiled=True).reshape(384, 128)  10.3 us
    pallas_call x1, Pallas kernels, corange_of(): pl.pallas_call(corange_kernel, in_specs=[ANY, ANY], out_specs=(VMEM, VMEM...  5.14 us
    ppermute x1, starting transfers between devices, per_device(): other = lax.ppermute(half, 'core', swap)  3.76 us
    ppermute x1, starting transfers between devices, per_device(): share_got = lax.ppermute(share_out, 'core', swap)  3.28 us
    pallas_call x1, Pallas kernels, gram_of(): pl.pallas_call(gram_kernel, in_specs=[VMEM, VMEM], out_specs=(VMEM, VMEM)...  3.23 us
  transfers between devices with their start and end apart: 3, of which 2 were waited for; matrix products, arithmetic and copies ran while one was open for 0% of the time, Pallas kernels for 4%

profile of v3, /device:TPU:1, one launch (start us, length us, event | category | flops | bytes accessed | tf_op | source)
XLA Modules:
  0.0 77.1 jit_solution(3881560529466176854)
XLA Ops:
  0.6 0.0 copy-start
  0.6 5.1 %shard_map.50 = (f32[16,96,128]{2,1,0:T(8,128)S(1)}, f32[16,96,128]{2,1,0:T(8,128)S(1)}, bf16[3072,512]{1,0:T(8,128)(2,1)S(1)}) custom-call(bf16[3072,512]{1,0:T(8,128)(2,1)} %x_hbm.1, bf16[3072,768]{1,0:T(8,128)(2,1)} %c_hbm.1), custom_call_target="tpu_custom_call" | custom-call | tf_op jit(solution)/shard_map/pallas_call | solution.py:80
  5.8 3.3 %collective-permute-start.1 = (f32[16,96,128]{2,1,0:T(8,128)S(1)}, f32[16,96,128]{2,1,0:T(8,128)S(1)}, u32[]{:S(2)}, u32[]{:S(2)}) collective-permute-start(f32[16,96,128]{2,1,0:T(8,128)S(1)} %get-tuple-element.15), channel_id=1, source_target_pairs={{0,16},{16,0},{1,17},{17,1},{2,18},{18,2},{3,19},{19,3},{4,20},{20... | collective-permute-start | bytes 2359304 | tf_op jit(solution)/shard_map/ppermute | solution.py:391
  9.1 0.0 copy-done
  9.1 3.2 %shard_map.51 = (f32[384,128]{1,0:T(8,128)S(1)}, f32[384,128]{1,0:T(8,128)S(1)}) custom-call(bf16[3072,512]{1,0:T(8,128)(2,1)S(1)} %get-tuple-element.11.x_ref.refs_4_, bf16[512,384]{1,0:T(8,128)(2,1)S(1)} %copy-done), custom_call_target="tpu_custom_call" | custom-call | tf_op jit(solution)/shard_map/pallas_call | solution.py:117
  12.3 0.1 collective-permute-start
  12.4 1.4 %collective-permute-done.gram_got = f32[384,128]{1,0:T(8,128)S(1)} collective-permute-done((f32[384,128]{1,0:T(8,128)S(1)}, f32[384,128]{1,0:T(8,128)S(1)}, u32[]{:S(2)}, u32[]{:S(2)}) %collective-permute-start) | collective-permute-done | bytes 196640 | tf_op jit(solution)/shard_map/ppermute | solution.py:393
  13.8 0.0 collective-permute-done.1.share_got
  13.8 0.1 shard_map.52
  13.9 20.7 %all_to_all.15.got_ref = f32[16,120,128]{2,1,0:T(8,128)S(1)} all-to-all(f32[16,120,128]{2,1,0:T(8,128)S(1)} %shard_map.52), channel_id=1, replica_groups=mesh['y'=4,'zl'=2,'core'=2,'zh'=4,'x'=4] {'y','x'}, dimensions={0} | all-to-all | bytes 1966080 | tf_op jit(solution)/shard_map/all_to_all | solution.py:395
  34.6 0.2 shard_map.53
  34.8 15.1 %all_to_all.16.got_ref = f32[8,40,128]{2,1,0:T(8,128)S(1)} all-to-all(f32[8,40,128]{2,1,0:T(8,128)S(1)} %shard_map.53), channel_id=1, replica_groups=mesh['y'=4,'zl'=2,'core'=2,'zh'=4,'x'=4] {'zl','zh'}, dimensions={0} | all-to-all | bytes 327680 | tf_op jit(solution)/shard_map/all_to_all | solution.py:396
  49.9 10.3 %all_to_all.17 = f32[16,24,128]{2,1,0:T(8,128)S(1)} all-to-all(f32[16,24,128]{2,1,0:T(8,128)S(1)} %get-tuple-element.16), channel_id=1, replica_groups=mesh['y'=4,'zl'=2,'core'=2,'zh'=4,'x'=4] {'y','x'}, dimensions={0} | all-to-all | bytes 393216 | tf_op jit(solution)/shard_map/all_to_all | solution.py:398
  60.2 3.8 %collective-permute-start.2 = (f32[384,128]{1,0:T(8,128)S(1)}, f32[384,128]{1,0:T(8,128)S(1)}, u32[]{:S(2)}, u32[]{:S(2)}) collective-permute-start(f32[384,128]{1,0:T(8,128)S(1)} %bitcast.2), channel_id=1, source_target_pairs={{0,16},{16,0},{1,17},{17,1},{2,18},{18,2},{3,19},{19,3},{4,20},{20... | collective-permute-start | bytes 589832 | tf_op jit(solution)/shard_map/ppermute | solution.py:399
  64.0 1.1 %collective-permute-done.2.refs_1_ = f32[384,128]{1,0:T(8,128)S(1)} collective-permute-done((f32[384,128]{1,0:T(8,128)S(1)}, f32[384,128]{1,0:T(8,128)S(1)}, u32[]{:S(2)}, u32[]{:S(2)}) %collective-permute-start.2) | collective-permute-done | bytes 196640 | tf_op jit(solution)/shard_map/ppermute | solution.py:399
  65.1 11.8 %shard_map.55 = (f32[3072,384]{1,0:T(8,128)}, f32[32,48]{1,0:T(8,128)}) custom-call(f32[384,128]{1,0:T(8,128)S(1)} %bitcast.3, f32[384,128]{1,0:T(8,128)S(1)} %collective-permute-done.2.refs_1_, f32[16,128]{1,0:T(8,128)S(1)} %get-tuple-element.17.refs_2_, bf16[512,384]{1,0:T(8,128)(2,1)S(1)} %copy-done, bf16[3072,512]{1,0:T(8,128)(2,1)S(1)} %get-tuple-element.11.x_ref.refs_4_), custom_call_target="tpu_custom_call" | custom-call | tf_op jit(solution)/shard_map/pallas_call | solution.py:368
  (1 shorter events, 0.0 us)
Async XLA Ops:
  0.6 8.4 %copy-start = (bf16[512,384]{1,0:T(8,128)(2,1)S(1)}, bf16[512,384]{1,0:T(8,128)(2,1)}, u32[]{:S(2)}) copy-start(bf16[512,384]{1,0:T(8,128)(2,1)} %refs_3_.1) | copy-start | bytes 1179652
  5.8 8.1 %collective-permute-start.1 = (f32[16,96,128]{2,1,0:T(8,128)S(1)}, f32[16,96,128]{2,1,0:T(8,128)S(1)}, u32[]{:S(2)}, u32[]{:S(2)}) collective-permute-start(f32[16,96,128]{2,1,0:T(8,128)S(1)} %get-tuple-element.15), channel_id=1, source_target_pairs={{0,16},{16,0},{1,17},{17,1},{2,18},{18,2},{3,19},{19,3},{4,20},{20... | collective-permute-start | bytes 2359304 | tf_op jit(solution)/shard_map/ppermute | solution.py:391
  12.3 1.5 %collective-permute-start = (f32[384,128]{1,0:T(8,128)S(1)}, f32[384,128]{1,0:T(8,128)S(1)}, u32[]{:S(2)}, u32[]{:S(2)}) collective-permute-start(f32[384,128]{1,0:T(8,128)S(1)} %get-tuple-element.13), channel_id=1, source_target_pairs={{0,16},{16,0},{1,17},{17,1},{2,18},{18,2},{3,19},{19,3},{4,20},{20... | collective-permute-start | bytes 589832 | tf_op jit(solution)/shard_map/ppermute | solution.py:393
  60.2 4.8 %collective-permute-start.2 = (f32[384,128]{1,0:T(8,128)S(1)}, f32[384,128]{1,0:T(8,128)S(1)}, u32[]{:S(2)}, u32[]{:S(2)}) collective-permute-start(f32[384,128]{1,0:T(8,128)S(1)} %bitcast.2), channel_id=1, source_target_pairs={{0,16},{16,0},{1,17},{17,1},{2,18},{18,2},{3,19},{19,3},{4,20},{20... | collective-permute-start | bytes 589832 | tf_op jit(solution)/shard_map/ppermute | solution.py:399

commit v4 on v3

--- a/solution.py
+++ b/solution.py
@@ -71,12 +71,14 @@
         for y in range(4):
             for n in range(4):
                 for zl in range(2):
-                    start = pl.multiple_of((y * 4 + zl * 2 + side) * 48, 8)
-                    ref[y * 4 + n, zl * 48 : 48 + zl * 48, :] = p_acc[n, pl.ds(start, 48), :]
+                    target = lax.rem(lax.axis_index("y") + y, 4)
+                    start = pl.multiple_of((target * 4 + zl * 2 + side) * 48, 8)
+                    at = (n * 2 + zl) * 48
+                    ref[y, at : at + 48, :] = p_acc[n, pl.ds(start, 48), :]
 
 
 def corange_of(x, c):
-    half = jax.ShapeDtypeStruct((16, 96, 128), F32)
+    half = jax.ShapeDtypeStruct((4, 384, 128), F32)
     return pl.pallas_call(
         corange_kernel,
         in_specs=[ANY, ANY],
@@ -124,73 +126,76 @@
     )(x, r)
 
 
-def pair_kernel(gram_ref, gram_got, share_ref, share_got, out_ref):
-    for peer in range(16):
-        at = pl.ds(peer * 24, 24)
-        out_ref[peer, 0:24, :] = gram_ref[at, :] + gram_got[at, :]
-        out_ref[peer, 24:120, :] = share_ref[peer] + share_got[peer]
-
-
-def pair_blocks(*args):
+def pair_kernel(share_ref, share_got, *shares):
+    for y, ref in enumerate(shares):
+        ref[...] = share_ref[y] + share_got[y]
+
+
+def pair_shares(*args):
+    share = jax.ShapeDtypeStruct((384, 128), F32)
     return pl.pallas_call(
         pair_kernel,
-        in_specs=[VMEM] * 4,
-        out_specs=VMEM,
-        out_shape=jax.ShapeDtypeStruct((16, 120, 128), F32),
+        in_specs=[VMEM] * 2,
+        out_specs=(VMEM,) * 4,
+        out_shape=(share,) * 4,
         compiler_params=pltpu.CompilerParams(vmem_limit_bytes=SUMS_VMEM),
     )(*args)
 
 
-def column_kernel(got_ref, out_ref):
+def column_kernel(got_ref, *refs):
     total = got_ref[0]
     for i in range(1, 16):
         total = total + got_ref[i]
-    gram = total[0:24]
-    shares = pltpu.roll(total[24:120], (4 - lax.axis_index("x")) % 4 * 32, 1)
-    lane = lanes((16, 128)) // 32
+    share = refs[0][...]
+    for ref in refs[1:4]:
+        share = share + ref[...]
+    out_ref = refs[4]
+    quarter = lanes((48, 128)) // 32
     for zl in range(2):
         for zh in range(4):
             peer = zl * 4 + zh
-            out_ref[peer, 0:24, :] = gram
-            out = jnp.zeros((16, 128), F32)
-            for q in range(3):
-                start = zl * 48 + q * 16
-                piece = shares[start : start + 16]
-                shift = ((q - zh) * 32) % 128
-                if shift:
-                    piece = pltpu.roll(piece, shift, 1)
-                out = jnp.where(lane == q, piece, out)
-            out_ref[peer, 24:40, :] = out
-
-
-def column_blocks(got):
+            out_ref[peer, 0:24, :] = total
+            out = share[zl * 48 : zl * 48 + 48]
+            for n in range(1, 4):
+                at = (n * 2 + zl) * 48
+                out = jnp.where(quarter == (n + zh) % 4, share[at : at + 48], out)
+            out_ref[peer, 24:72, :] = out
+
+
+def column_blocks(*args):
     return pl.pallas_call(
         column_kernel,
-        in_specs=[VMEM],
+        in_specs=[VMEM] * 5,
         out_specs=VMEM,
-        out_shape=jax.ShapeDtypeStruct((8, 40, 128), F32),
+        out_shape=jax.ShapeDtypeStruct((8, 72, 128), F32),
         compiler_params=pltpu.CompilerParams(vmem_limit_bytes=SUMS_VMEM),
-    )(got)
-
-
-def plane_kernel(got_ref, gram_ref, share_ref):
+    )(*args)
+
+
+def plane_kernel(got_ref, out_ref):
     total = got_ref[0]
     for i in range(1, 8):
         total = total + got_ref[i]
-    for i in range(16):
-        gram_ref[i] = total[0:24]
-    share_ref[...] = total[24:40]
+    shares = pltpu.roll(total[24:72], (4 - lax.axis_index("zh")) % 4 * 32, 1)
+    group = lanes((16, 128)) // 32
+    for n in range(4):
+        out = jnp.zeros((16, 128), F32)
+        for q in range(3):
+            piece = shares[q * 16 : q * 16 + 16]
+            if q != n:
+                piece = pltpu.roll(piece, (q - n) % 4 * 32, 1)
+            out = jnp.where(group == q, piece, out)
+        for y in range(4):
+            out_ref[y * 4 + n, 0:24, :] = total[0:24]
+            out_ref[y * 4 + n, 24:40, :] = out
 
 
 def plane_blocks(got):
     return pl.pallas_call(
         plane_kernel,
         in_specs=[VMEM],
-        out_specs=(VMEM, VMEM),
-        out_shape=(
-            jax.ShapeDtypeStruct((16, 24, 128), F32),
-            jax.ShapeDtypeStruct((16, 128), F32),
-        ),
+        out_specs=VMEM,
+        out_shape=jax.ShapeDtypeStruct((16, 40, 128), F32),
         compiler_params=pltpu.CompilerParams(vmem_limit_bytes=SUMS_VMEM),
     )(got)
 
@@ -201,10 +206,9 @@
 
 def inverse_factor(block, same, beside=None):
     n, half = 16, 8
-    d = [block[8 * i : 8 * i + 8, :] for i in range(n)]
+    e = [block[8 * i : 8 * i + 8, :] for i in range(n)]
     row = lax.broadcasted_iota(jnp.int32, (8, 128), 0)
     lane = lanes((8, 128))
-    v = [jnp.where(lane == row + 8 * i, 1.0, 0.0).astype(F32) for i in range(n)]
 
     def stacked(rows):
         out = rows[0]
@@ -213,24 +217,20 @@
         return out
 
     def columns_of(k, p):
-        return [spread(d[k][:, 8 * p + j : 8 * p + j + 1]) for j in range(8)]
+        return [spread(e[k][:, 8 * p + j : 8 * p + j + 1]) for j in range(8)]
 
     def reader(values, at):
         for j, value in enumerate(values):
             same[at + 8 * j : at + 8 * j + 8, :] = value
         return lambda j, k: same[pl.ds(at + 8 * j + k, 8, stride=0), :]
 
-    def rows_of(value, at):
-        read = reader([value], at)
-        return [read(0, j) for j in range(8)]
-
-    own, u = columns_of(0, 0), []
+    own = columns_of(0, 0)
     for p in range(n):
         base = (p % 2) * 160
         read = reader(own, base)
         s = [[read(j, k) if k >= j else None for j in range(8)] for k in range(8)]
-        last = p == n - 1
-        ahead = not last and p != half - 1
+        here = (lane >= 8 * p) & (lane < 8 * p + 8)
+        ahead = p != n - 1 and p != half - 1
         if ahead:
             below, own = columns_of(p + 1, p), columns_of(p + 1, p + 1)
         r = []
@@ -257,40 +257,44 @@
             for m in range(8):
                 for j in range(8):
                     own[m] = own[m] - below[j] * read(j, m)
-        vx = forward(rows_of(v[p], base + 128))
-        v[p] = stacked(vx)
-        if not last:
-            dx = forward(rows_of(d[p], base + 136))
-            u.append(stacked(dx))
+        read = reader([jnp.where(here, jnp.where(lane == row + 8 * p, 1.0, 0.0), e[p])], base + 128)
+        ex = forward([read(0, j) for j in range(8)])
+        e[p] = stacked(ex)
         if beside is not None:
             beside(p)
         for k in range(p + 1, half if p < half else n):
             factors = below if k == p + 1 else forward(columns_of(k, p))
+            e[k] = jnp.where(here, 0.0, e[k])
             for j in range(8):
-                d[k] = d[k] - factors[j] * dx[j]
-                v[k] = v[k] - factors[j] * vx[j]
+                e[k] = e[k] - factors[j] * ex[j]
         if p == half - 1:
-            top = jnp.concatenate(u, axis=0)
-            both = jnp.where(lanes((64, 128)) < 64, jnp.concatenate(v[:half], axis=0), top)
-            minus = exact(top, both, CONTRACT0)
+            top = jnp.concatenate(
+                [jnp.where((lane > 8 * i + 7) & (lane < 64), 0.0, e[i]) for i in range(half)], axis=0
+            )
+            minus = exact(top, top, CONTRACT0)
             for k in range(half, n):
-                part = minus[8 * k : 8 * k + 8]
-                d[k] = d[k] - part
-                v[k] = jnp.where(lane < 64, -part, v[k])
+                e[k] = jnp.where(lane < 64, 0.0, e[k]) - minus[8 * k : 8 * k + 8]
             own = columns_of(half, half)
-    return jnp.concatenate(v, axis=0)
+    return jnp.concatenate([jnp.where(lane > 8 * i + 7, 0.0, e[i]) for i in range(n)], axis=0)
 
 
 def exact(a, b, contract=(((1,), (0,)), ((), ()))):
     return lax.dot_general(a, b, contract, precision=lax.Precision.HIGHEST, preferred_element_type=F32)
 
 
-def basis_kernel(scale, a_ref, b_ref, share_ref, r_ref, x_ref, out_hbm, cosketch_ref, g, out_vmem, y_ref, same, out_sem):
+def basis_kernel(scale, a_ref, b_ref, got_ref, r_ref, x_ref, out_hbm, cosketch_hbm, g, out_vmem, y_ref, same, cosketch, cosketch_sem, out_sem):
     core = lax.axis_index("core")
     g[pl.ds(pl.multiple_of(core * 384, 8), 384), :] = a_ref[...]
     g[pl.ds(pl.multiple_of((1 - core) * 384, 8), 384), :] = b_ref[...]
     rows = x_ref.shape[0]
-    stores = []
+    y = lax.axis_index("y")
+    share = got_ref[y * 4, 24:40, :]
+    for n in range(1, 4):
+        share = share + got_ref[y * 4 + n, 24:40, :]
+    turned = [share, pltpu.roll(share, 96, 1), pltpu.roll(share, 64, 1)]
+    cosketch[...] = jnp.concatenate(turned, axis=0).T[0:32, :]
+    stores = [pltpu.make_async_copy(cosketch, cosketch_hbm, cosketch_sem)]
+    stores[0].start()
 
     def block(i):
         return g[i * 128 : (i + 1) * 128, :]
@@ -323,14 +327,11 @@
         at = pl.ds(start, size)
         stores.append(
             pltpu.make_async_copy(
-                out_vmem.at[i, at, :], out_hbm.at[at, pl.ds(i * 128, 128)], out_sem.at[len(stores)]
+                out_vmem.at[i, at, :], out_hbm.at[at, pl.ds(i * 128, 128)], out_sem.at[len(stores) - 1]
             )
         )
         stores[-1].start()
 
-    share = share_ref[...]
-    turned = [share, pltpu.roll(share, 96, 1), pltpu.roll(share, 64, 1)]
-    cosketch_ref[...] = jnp.concatenate(turned, axis=0).T[0:32, :]
     m0 = inverse_factor(block(0), same)
     row0 = exact(m0, jnp.concatenate([block(1), block(2)], axis=1))
     minus = exact(row0, row0, CONTRACT0)
@@ -364,11 +365,11 @@
         copy.wait()
 
 
-def basis_of(scale, a, b, share, r, x):
+def basis_of(scale, a, b, got, r, x):
     return pl.pallas_call(
         lambda *refs: basis_kernel(scale, *refs),
         in_specs=[VMEM] * 5,
-        out_specs=(ANY, VMEM),
+        out_specs=(ANY, ANY),
         out_shape=(
             jax.ShapeDtypeStruct((x.shape[0], 384), F32),
             jax.ShapeDtypeStruct((32, 48), F32),
@@ -378,10 +379,12 @@
             pltpu.VMEM((3, x.shape[0], 128), F32),
             pltpu.VMEM((x.shape[0], 256), BF16),
             pltpu.VMEM((320, 128), F32),
+            pltpu.VMEM((32, 48), F32),
+            pltpu.SemaphoreType.DMA,
             pltpu.SemaphoreType.DMA((8,)),
         ],
         compiler_params=pltpu.CompilerParams(vmem_limit_bytes=BASIS_VMEM),
-    )(a, b, share, r, x)
+    )(a, b, got, r, x)
 
 
 def per_device(snapshots, range_test, corange_test):
@@ -391,13 +394,16 @@
     share_got = lax.ppermute(share_out, "core", swap)
     gram, gram_out = gram_of(held, range_test)
     gram_got = lax.ppermute(gram_out, "core", swap)
-    pair = pair_blocks(gram, gram_got, share, share_got)
+    shares = list(pair_shares(share, share_got))
+    for shift in range(1, 4):
+        shares[shift] = lax.ppermute(shares[shift], "y", [(y, (y + shift) % 4) for y in range(4)])
+    pair = (gram + gram_got).reshape(16, 24, 128)
     got = lax.all_to_all(pair, PLANE, 0, 0, tiled=True)
-    got = lax.all_to_all(column_blocks(got), COLUMN, 0, 0, tiled=True)
-    gram, share = plane_blocks(got)
-    half = lax.all_to_all(gram, PLANE, 0, 0, tiled=True).reshape(384, 128)
+    got = lax.all_to_all(column_blocks(got, *shares), COLUMN, 0, 0, tiled=True)
+    got = lax.all_to_all(plane_blocks(got), PLANE, 0, 0, tiled=True)
+    half = got[:, :24].reshape(384, 128)
     other = lax.ppermute(half, "core", swap)
-    basis, cosketch = basis_of(float(total) ** 0.5, half, other, share, range_test, held)
+    basis, cosketch = basis_of(float(total) ** 0.5, half, other, got, range_test, held)
     return basis, cosketch.T
 
 

time: 77.3 us -> 75.2 us (0.973)
  starting transfers between devices: 7.16 us -> 10.9 us
  blocking collectives: 46.1 us -> 42.8 us
  waiting for transfers between devices: 2.49 us -> 1.08 us
  Pallas kernels: 20.5 us -> 19.3 us
    all_to_all x1, blocking collectives: 20.7 us -> 11.3 us  [per_device(): got = lax.all_to_all(pair, PLANE, 0, 0, tiled=True)]
    all_to_all x2, blocking collectives: 25.4 us -> 31.5 us  [the longest x1 17.6 us: per_device(): got = lax.all_to_all(column_blocks(got, *shares), COLUMN, 0, 0, tiled=True)]
    ppermute x0 -> x3, starting transfers between devices: none -> 3.32 us  [per_device(): lax.ppermute(shares[shift], 'y', [(y, (y + shift) % 4) for y in range(4)])]
    ppermute x1, waiting for transfers between devices: 1.41 us -> 0.01 us  [per_device(): gram_got = lax.ppermute(gram_out, 'core', swap)]
    pallas_call x1, Pallas kernels: 11.8 us -> 10.7 us  [basis_of(): pl.pallas_call(lambda *refs: basis_kernel(scale, *refs), in_specs=[VMEM]...]
  transfers between devices with their start and end apart: 3 -> 6, of which waited for: 2 -> 1; matrix products, arithmetic and copies ran while one was open for 0% -> 0% of each run, Pallas kernels for 4% -> 4%
where the time goes in v4:
time: 75.2 us; the launch traced here: 75 us
  blocking collectives  42.8 us (57%)
  Pallas kernels  19.3 us (26%)
  starting transfers between devices  10.9 us (14%)
  waiting for transfers between devices  1.08 us (1%)
  between operations  0.86 us (1%)
    all_to_all x1, blocking collectives, per_device(): got = lax.all_to_all(column_blocks(got, *shares), COLUMN, 0, 0, tiled=True)  17.6 us
    all_to_all x1, blocking collectives, per_device(): got = lax.all_to_all(plane_blocks(got), PLANE, 0, 0, tiled=True)  13.9 us
    all_to_all x1, blocking collectives, per_device(): got = lax.all_to_all(pair, PLANE, 0, 0, tiled=True)  11.3 us
    pallas_call x1, Pallas kernels, basis_of(): pl.pallas_call(lambda *refs: basis_kernel(scale, *refs), in_specs=[VMEM]...  10.7 us
    pallas_call x1, Pallas kernels, corange_of(): pl.pallas_call(corange_kernel, in_specs=[ANY, ANY], out_specs=(VMEM, VMEM...  5.09 us
    ppermute x1, starting transfers between devices, per_device(): other = lax.ppermute(half, 'core', swap)  4.12 us
    ppermute x1, starting transfers between devices, per_device(): share_got = lax.ppermute(share_out, 'core', swap)  3.32 us
    ppermute x3, starting transfers between devices, per_device(): lax.ppermute(shares[shift], 'y', [(y, (y + shift) % 4) for y in range(4)])  3.32 us
  transfers between devices with their start and end apart: 6, of which 1 were waited for; matrix products, arithmetic and copies ran while one was open for 0% of the time, Pallas kernels for 4%

profile of v4, /device:TPU:1, one launch (start us, length us, event | category | flops | bytes accessed | tf_op | source)
XLA Modules:
  0.0 75.0 jit_solution(14584598771195641857)
XLA Ops:
  0.6 0.0 copy-start
  0.6 5.1 %shard_map.50 = (f32[4,384,128]{2,1,0:T(8,128)S(1)}, f32[4,384,128]{2,1,0:T(8,128)S(1)}, bf16[3072,512]{1,0:T(8,128)(2,1)S(1)}) custom-call(bf16[3072,512]{1,0:T(8,128)(2,1)} %x_hbm.1, bf16[3072,768]{1,0:T(8,128)(2,1)} %c_hbm.1), custom_call_target="tpu_custom_call" | custom-call | tf_op jit(solution)/shard_map/pallas_call | solution.py:82
  5.7 3.3 %collective-permute-start.1 = (f32[4,384,128]{2,1,0:T(8,128)S(1)}, f32[4,384,128]{2,1,0:T(8,128)S(1)}, u32[]{:S(2)}, u32[]{:S(2)}) collective-permute-start(f32[4,384,128]{2,1,0:T(8,128)S(1)} %get-tuple-element.17), channel_id=1, source_target_pairs={{0,16},{16,0},{1,17},{17,1},{2,18},{18,2},{3,19},{19,3},{4,20},{20... | collective-permute-start | bytes 2359304 | tf_op jit(solution)/shard_map/ppermute | solution.py:394
  9.1 0.0 copy-done
  9.1 3.2 %shard_map.51 = (f32[384,128]{1,0:T(8,128)S(1)}, f32[384,128]{1,0:T(8,128)S(1)}) custom-call(bf16[3072,512]{1,0:T(8,128)(2,1)S(1)} %get-tuple-element.13.x_ref.refs_4_, bf16[512,384]{1,0:T(8,128)(2,1)S(1)} %copy-done), custom_call_target="tpu_custom_call" | custom-call | tf_op jit(solution)/shard_map/pallas_call | solution.py:119
  12.3 0.1 collective-permute-start
  12.4 0.0 collective-permute-done.1.share_got
  12.4 0.1 shard_map.52
  12.5 0.1 collective-permute-start.2
  12.6 2.2 %collective-permute-start.3 = (f32[384,128]{1,0:T(8,128)S(1)}, f32[384,128]{1,0:T(8,128)S(1)}, u32[]{:S(2)}, u32[]{:S(2)}) collective-permute-start(f32[384,128]{1,0:T(8,128)S(1)} %get-tuple-element.20), channel_id=1, source_target_pairs={{0,128},{64,192},{128,0},{192,64},{1,129},{65,193},{129,1},{193,65... | collective-permute-start | bytes 589832 | tf_op jit(solution)/shard_map/ppermute | solution.py:399
  14.8 1.1 %collective-permute-start.4 = (f32[384,128]{1,0:T(8,128)S(1)}, f32[384,128]{1,0:T(8,128)S(1)}, u32[]{:S(2)}, u32[]{:S(2)}) collective-permute-start(f32[384,128]{1,0:T(8,128)S(1)} %get-tuple-element.21), channel_id=1, source_target_pairs={{0,192},{64,0},{128,64},{192,128},{1,193},{65,1},{129,65},{193,129... | collective-permute-start | bytes 589832 | tf_op jit(solution)/shard_map/ppermute | solution.py:399
  15.8 0.0 collective-permute-done
  15.9 11.3 %all_to_all.15.got_ref = f32[16,24,128]{2,1,0:T(8,128)S(1)} all-to-all(f32[16,24,128]{2,1,0:T(8,128)S(1)} %bitcast.5), channel_id=1, replica_groups=mesh['y'=4,'zl'=2,'core'=2,'zh'=4,'x'=4] {'y','x'}, dimensions={0} | all-to-all | bytes 393216 | tf_op jit(solution)/shard_map/all_to_all | solution.py:401
  27.2 0.0 collective-permute-done.2.refs_1_
  27.2 0.0 collective-permute-done.3.refs_2_
  27.2 0.0 collective-permute-done.4.refs_3_
  27.2 0.1 shard_map.53
  27.3 17.6 %all_to_all.16.got_ref = f32[8,72,128]{2,1,0:T(8,128)S(1)} all-to-all(f32[8,72,128]{2,1,0:T(8,128)S(1)} %shard_map.53), channel_id=1, replica_groups=mesh['y'=4,'zl'=2,'core'=2,'zh'=4,'x'=4] {'zl','zh'}, dimensions={0} | all-to-all | bytes 589824 | tf_op jit(solution)/shard_map/all_to_all | solution.py:402
  44.9 0.2 shard_map.54
  45.1 13.9 %all_to_all.17.refs_2_ = f32[16,40,128]{2,1,0:T(8,128)S(1)} all-to-all(f32[16,40,128]{2,1,0:T(8,128)S(1)} %shard_map.54), channel_id=1, replica_groups=mesh['y'=4,'zl'=2,'core'=2,'zh'=4,'x'=4] {'y','x'}, dimensions={0} | all-to-all | bytes 655360 | tf_op jit(solution)/shard_map/all_to_all | solution.py:403
  59.0 4.1 %collective-permute-start.5 = (f32[384,128]{1,0:T(8,128)S(1)}, f32[384,128]{1,0:T(8,128)S(1)}, u32[]{:S(2)}, u32[]{:S(2)}) collective-permute-start(f32[384,128]{1,0:T(8,128)S(1)} %bitcast.3), channel_id=1, source_target_pairs={{0,16},{16,0},{1,17},{17,1},{2,18},{18,2},{3,19},{19,3},{4,20},{20... | collective-permute-start | bytes 589832 | tf_op jit(solution)/shard_map/ppermute | solution.py:405
  63.1 1.1 %collective-permute-done.5.refs_1_ = f32[384,128]{1,0:T(8,128)S(1)} collective-permute-done((f32[384,128]{1,0:T(8,128)S(1)}, f32[384,128]{1,0:T(8,128)S(1)}, u32[]{:S(2)}, u32[]{:S(2)}) %collective-permute-start.5) | collective-permute-done | bytes 196640 | tf_op jit(solution)/shard_map/ppermute | solution.py:405
  64.2 10.7 %shard_map.55 = (f32[3072,384]{1,0:T(8,128)}, f32[32,48]{1,0:T(8,128)}) custom-call(f32[384,128]{1,0:T(8,128)S(1)} %bitcast.4, f32[384,128]{1,0:T(8,128)S(1)} %collective-permute-done.5.refs_1_, f32[16,40,128]{2,1,0:T(8,128)S(1)} %all_to_all.17.refs_2_, bf16[512,384]{1,0:T(8,128)(2,1)S(1)} %copy-done, bf16[3072,512]{1,0:T(8,128)(2,1)S(1)} %get-tuple-element.13.x_ref.refs_4_), custom_call_target="tpu_custom_call" | custom-call | tf_op jit(solution)/shard_map/pallas_call | solution.py:369
  (2 shorter events, 0.0 us)
Async XLA Ops:
  0.6 8.4 %copy-start = (bf16[512,384]{1,0:T(8,128)(2,1)S(1)}, bf16[512,384]{1,0:T(8,128)(2,1)}, u32[]{:S(2)}) copy-start(bf16[512,384]{1,0:T(8,128)(2,1)} %refs_3_.1) | copy-start | bytes 1179652
  5.7 6.7 %collective-permute-start.1 = (f32[4,384,128]{2,1,0:T(8,128)S(1)}, f32[4,384,128]{2,1,0:T(8,128)S(1)}, u32[]{:S(2)}, u32[]{:S(2)}) collective-permute-start(f32[4,384,128]{2,1,0:T(8,128)S(1)} %get-tuple-element.17), channel_id=1, source_target_pairs={{0,16},{16,0},{1,17},{17,1},{2,18},{18,2},{3,19},{19,3},{4,20},{20... | collective-permute-start | bytes 2359304 | tf_op jit(solution)/shard_map/ppermute | solution.py:394
  12.3 3.5 %collective-permute-start = (f32[384,128]{1,0:T(8,128)S(1)}, f32[384,128]{1,0:T(8,128)S(1)}, u32[]{:S(2)}, u32[]{:S(2)}) collective-permute-start(f32[384,128]{1,0:T(8,128)S(1)} %get-tuple-element.15), channel_id=1, source_target_pairs={{0,16},{16,0},{1,17},{17,1},{2,18},{18,2},{3,19},{19,3},{4,20},{20... | collective-permute-start | bytes 589832 | tf_op jit(solution)/shard_map/ppermute | solution.py:396
  12.5 14.7 %collective-permute-start.2 = (f32[384,128]{1,0:T(8,128)S(1)}, f32[384,128]{1,0:T(8,128)S(1)}, u32[]{:S(2)}, u32[]{:S(2)}) collective-permute-start(f32[384,128]{1,0:T(8,128)S(1)} %get-tuple-element.19), channel_id=1, source_target_pairs={{0,64},{64,128},{128,192},{192,0},{1,65},{65,129},{129,193},{193,1... | collective-permute-start | bytes 589832 | tf_op jit(solution)/shard_map/ppermute | solution.py:399
  12.6 14.6 %collective-permute-start.3 = (f32[384,128]{1,0:T(8,128)S(1)}, f32[384,128]{1,0:T(8,128)S(1)}, u32[]{:S(2)}, u32[]{:S(2)}) collective-permute-start(f32[384,128]{1,0:T(8,128)S(1)} %get-tuple-element.20), channel_id=1, source_target_pairs={{0,128},{64,192},{128,0},{192,64},{1,129},{65,193},{129,1},{193,65... | collective-permute-start | bytes 589832 | tf_op jit(solution)/shard_map/ppermute | solution.py:399
  14.8 12.4 %collective-permute-start.4 = (f32[384,128]{1,0:T(8,128)S(1)}, f32[384,128]{1,0:T(8,128)S(1)}, u32[]{:S(2)}, u32[]{:S(2)}) collective-permute-start(f32[384,128]{1,0:T(8,128)S(1)} %get-tuple-element.21), channel_id=1, source_target_pairs={{0,192},{64,0},{128,64},{192,128},{1,193},{65,1},{129,65},{193,129... | collective-permute-start | bytes 589832 | tf_op jit(solution)/shard_map/ppermute | solution.py:399
  59.0 5.2 %collective-permute-start.5 = (f32[384,128]{1,0:T(8,128)S(1)}, f32[384,128]{1,0:T(8,128)S(1)}, u32[]{:S(2)}, u32[]{:S(2)}) collective-permute-start(f32[384,128]{1,0:T(8,128)S(1)} %bitcast.3), channel_id=1, source_target_pairs={{0,16},{16,0},{1,17},{17,1},{2,18},{18,2},{3,19},{19,3},{4,20},{20... | collective-permute-start | bytes 589832 | tf_op jit(solution)/shard_map/ppermute | solution.py:405

commit v5 on v4

--- a/solution.py
+++ b/solution.py
@@ -356,8 +356,8 @@
     weight = jnp.concatenate(
         [jnp.concatenate([high, low], axis=1), jnp.concatenate([high, jnp.zeros_like(low)], axis=1)], axis=0
     )
-    size = rows // 4
-    for p in range(4):
+    size = rows // 6
+    for p in range(6):
         at = pl.ds(p * size, size)
         out_vmem[2, at, :] = times(y_ref[at, :], weight)
         store(2, p * size, size)
@@ -381,7 +381,7 @@
             pltpu.VMEM((320, 128), F32),
             pltpu.VMEM((32, 48), F32),
             pltpu.SemaphoreType.DMA,
-            pltpu.SemaphoreType.DMA((8,)),
+            pltpu.SemaphoreType.DMA((10,)),
         ],
         compiler_params=pltpu.CompilerParams(vmem_limit_bytes=BASIS_VMEM),
     )(a, b, got, r, x)

time: 75.2 us -> 75.2 us (level)
  no operation moved by 1% of the time
where the time goes in v5:
time: 75.2 us; the launch traced here: 75 us
  blocking collectives  42.8 us (57%)
  Pallas kernels  19.3 us (26%)
  starting transfers between devices  10.9 us (14%)
  waiting for transfers between devices  1.08 us (1%)
  between operations  0.86 us (1%)
    all_to_all x1, blocking collectives, per_device(): got = lax.all_to_all(column_blocks(got, *shares), COLUMN, 0, 0, tiled=True)  17.6 us
    all_to_all x1, blocking collectives, per_device(): got = lax.all_to_all(plane_blocks(got), PLANE, 0, 0, tiled=True)  13.9 us
    all_to_all x1, blocking collectives, per_device(): got = lax.all_to_all(pair, PLANE, 0, 0, tiled=True)  11.3 us
    pallas_call x1, Pallas kernels, basis_of(): pl.pallas_call(lambda *refs: basis_kernel(scale, *refs), in_specs=[VMEM]...  10.6 us
    pallas_call x1, Pallas kernels, corange_of(): pl.pallas_call(corange_kernel, in_specs=[ANY, ANY], out_specs=(VMEM, VMEM...  5.09 us
    ppermute x1, starting transfers between devices, per_device(): other = lax.ppermute(half, 'core', swap)  4.12 us
    ppermute x1, starting transfers between devices, per_device(): share_got = lax.ppermute(share_out, 'core', swap)  3.32 us
    ppermute x3, starting transfers between devices, per_device(): lax.ppermute(shares[shift], 'y', [(y, (y + shift) % 4) for y in range(4)])  3.32 us
  transfers between devices with their start and end apart: 6, of which 1 were waited for; matrix products, arithmetic and copies ran while one was open for 0% of the time, Pallas kernels for 4%

profile of v5, /device:TPU:1, one launch (start us, length us, event | category | flops | bytes accessed | tf_op | source)
XLA Modules:
  0.0 75.0 jit_solution(5025558242772292841)
XLA Ops:
  0.6 0.0 copy-start
  0.6 5.1 %shard_map.50 = (f32[4,384,128]{2,1,0:T(8,128)S(1)}, f32[4,384,128]{2,1,0:T(8,128)S(1)}, bf16[3072,512]{1,0:T(8,128)(2,1)S(1)}) custom-call(bf16[3072,512]{1,0:T(8,128)(2,1)} %x_hbm.1, bf16[3072,768]{1,0:T(8,128)(2,1)} %c_hbm.1), custom_call_target="tpu_custom_call" | custom-call | tf_op jit(solution)/shard_map/pallas_call | solution.py:82
  5.7 3.3 %collective-permute-start.1 = (f32[4,384,128]{2,1,0:T(8,128)S(1)}, f32[4,384,128]{2,1,0:T(8,128)S(1)}, u32[]{:S(2)}, u32[]{:S(2)}) collective-permute-start(f32[4,384,128]{2,1,0:T(8,128)S(1)} %get-tuple-element.17), channel_id=1, source_target_pairs={{0,16},{16,0},{1,17},{17,1},{2,18},{18,2},{3,19},{19,3},{4,20},{20... | collective-permute-start | bytes 2359304 | tf_op jit(solution)/shard_map/ppermute | solution.py:394
  9.1 0.0 copy-done
  9.1 3.2 %shard_map.51 = (f32[384,128]{1,0:T(8,128)S(1)}, f32[384,128]{1,0:T(8,128)S(1)}) custom-call(bf16[3072,512]{1,0:T(8,128)(2,1)S(1)} %get-tuple-element.13.x_ref.refs_4_, bf16[512,384]{1,0:T(8,128)(2,1)S(1)} %copy-done), custom_call_target="tpu_custom_call" | custom-call | tf_op jit(solution)/shard_map/pallas_call | solution.py:119
  12.3 0.1 collective-permute-start
  12.4 0.0 collective-permute-done.1.share_got
  12.4 0.1 shard_map.52
  12.5 0.1 collective-permute-start.2
  12.6 2.2 %collective-permute-start.3 = (f32[384,128]{1,0:T(8,128)S(1)}, f32[384,128]{1,0:T(8,128)S(1)}, u32[]{:S(2)}, u32[]{:S(2)}) collective-permute-start(f32[384,128]{1,0:T(8,128)S(1)} %get-tuple-element.20), channel_id=1, source_target_pairs={{0,128},{64,192},{128,0},{192,64},{1,129},{65,193},{129,1},{193,65... | collective-permute-start | bytes 589832 | tf_op jit(solution)/shard_map/ppermute | solution.py:399
  14.8 1.1 %collective-permute-start.4 = (f32[384,128]{1,0:T(8,128)S(1)}, f32[384,128]{1,0:T(8,128)S(1)}, u32[]{:S(2)}, u32[]{:S(2)}) collective-permute-start(f32[384,128]{1,0:T(8,128)S(1)} %get-tuple-element.21), channel_id=1, source_target_pairs={{0,192},{64,0},{128,64},{192,128},{1,193},{65,1},{129,65},{193,129... | collective-permute-start | bytes 589832 | tf_op jit(solution)/shard_map/ppermute | solution.py:399
  15.8 0.0 collective-permute-done
  15.9 11.3 %all_to_all.15.got_ref = f32[16,24,128]{2,1,0:T(8,128)S(1)} all-to-all(f32[16,24,128]{2,1,0:T(8,128)S(1)} %bitcast.5), channel_id=1, replica_groups=mesh['y'=4,'zl'=2,'core'=2,'zh'=4,'x'=4] {'y','x'}, dimensions={0} | all-to-all | bytes 393216 | tf_op jit(solution)/shard_map/all_to_all | solution.py:401
  27.2 0.0 collective-permute-done.2.refs_1_
  27.2 0.0 collective-permute-done.3.refs_2_
  27.2 0.0 collective-permute-done.4.refs_3_
  27.2 0.1 shard_map.53
  27.3 17.6 %all_to_all.16.got_ref = f32[8,72,128]{2,1,0:T(8,128)S(1)} all-to-all(f32[8,72,128]{2,1,0:T(8,128)S(1)} %shard_map.53), channel_id=1, replica_groups=mesh['y'=4,'zl'=2,'core'=2,'zh'=4,'x'=4] {'zl','zh'}, dimensions={0} | all-to-all | bytes 589824 | tf_op jit(solution)/shard_map/all_to_all | solution.py:402
  44.9 0.2 shard_map.54
  45.1 13.9 %all_to_all.17.refs_2_ = f32[16,40,128]{2,1,0:T(8,128)S(1)} all-to-all(f32[16,40,128]{2,1,0:T(8,128)S(1)} %shard_map.54), channel_id=1, replica_groups=mesh['y'=4,'zl'=2,'core'=2,'zh'=4,'x'=4] {'y','x'}, dimensions={0} | all-to-all | bytes 655360 | tf_op jit(solution)/shard_map/all_to_all | solution.py:403
  59.0 4.1 %collective-permute-start.5 = (f32[384,128]{1,0:T(8,128)S(1)}, f32[384,128]{1,0:T(8,128)S(1)}, u32[]{:S(2)}, u32[]{:S(2)}) collective-permute-start(f32[384,128]{1,0:T(8,128)S(1)} %bitcast.3), channel_id=1, source_target_pairs={{0,16},{16,0},{1,17},{17,1},{2,18},{18,2},{3,19},{19,3},{4,20},{20... | collective-permute-start | bytes 589832 | tf_op jit(solution)/shard_map/ppermute | solution.py:405
  63.1 1.1 %collective-permute-done.5.refs_1_ = f32[384,128]{1,0:T(8,128)S(1)} collective-permute-done((f32[384,128]{1,0:T(8,128)S(1)}, f32[384,128]{1,0:T(8,128)S(1)}, u32[]{:S(2)}, u32[]{:S(2)}) %collective-permute-start.5) | collective-permute-done | bytes 196640 | tf_op jit(solution)/shard_map/ppermute | solution.py:405
  64.2 10.6 %shard_map.55 = (f32[3072,384]{1,0:T(8,128)}, f32[32,48]{1,0:T(8,128)}) custom-call(f32[384,128]{1,0:T(8,128)S(1)} %bitcast.4, f32[384,128]{1,0:T(8,128)S(1)} %collective-permute-done.5.refs_1_, f32[16,40,128]{2,1,0:T(8,128)S(1)} %all_to_all.17.refs_2_, bf16[512,384]{1,0:T(8,128)(2,1)S(1)} %copy-done, bf16[3072,512]{1,0:T(8,128)(2,1)S(1)} %get-tuple-element.13.x_ref.refs_4_), custom_call_target="tpu_custom_call" | custom-call | tf_op jit(solution)/shard_map/pallas_call | solution.py:369
  (2 shorter events, 0.0 us)
Async XLA Ops:
  0.6 8.4 %copy-start = (bf16[512,384]{1,0:T(8,128)(2,1)S(1)}, bf16[512,384]{1,0:T(8,128)(2,1)}, u32[]{:S(2)}) copy-start(bf16[512,384]{1,0:T(8,128)(2,1)} %refs_3_.1) | copy-start | bytes 1179652
  5.7 6.7 %collective-permute-start.1 = (f32[4,384,128]{2,1,0:T(8,128)S(1)}, f32[4,384,128]{2,1,0:T(8,128)S(1)}, u32[]{:S(2)}, u32[]{:S(2)}) collective-permute-start(f32[4,384,128]{2,1,0:T(8,128)S(1)} %get-tuple-element.17), channel_id=1, source_target_pairs={{0,16},{16,0},{1,17},{17,1},{2,18},{18,2},{3,19},{19,3},{4,20},{20... | collective-permute-start | bytes 2359304 | tf_op jit(solution)/shard_map/ppermute | solution.py:394
  12.3 3.5 %collective-permute-start = (f32[384,128]{1,0:T(8,128)S(1)}, f32[384,128]{1,0:T(8,128)S(1)}, u32[]{:S(2)}, u32[]{:S(2)}) collective-permute-start(f32[384,128]{1,0:T(8,128)S(1)} %get-tuple-element.15), channel_id=1, source_target_pairs={{0,16},{16,0},{1,17},{17,1},{2,18},{18,2},{3,19},{19,3},{4,20},{20... | collective-permute-start | bytes 589832 | tf_op jit(solution)/shard_map/ppermute | solution.py:396
  12.5 14.7 %collective-permute-start.2 = (f32[384,128]{1,0:T(8,128)S(1)}, f32[384,128]{1,0:T(8,128)S(1)}, u32[]{:S(2)}, u32[]{:S(2)}) collective-permute-start(f32[384,128]{1,0:T(8,128)S(1)} %get-tuple-element.19), channel_id=1, source_target_pairs={{0,64},{64,128},{128,192},{192,0},{1,65},{65,129},{129,193},{193,1... | collective-permute-start | bytes 589832 | tf_op jit(solution)/shard_map/ppermute | solution.py:399
  12.6 14.6 %collective-permute-start.3 = (f32[384,128]{1,0:T(8,128)S(1)}, f32[384,128]{1,0:T(8,128)S(1)}, u32[]{:S(2)}, u32[]{:S(2)}) collective-permute-start(f32[384,128]{1,0:T(8,128)S(1)} %get-tuple-element.20), channel_id=1, source_target_pairs={{0,128},{64,192},{128,0},{192,64},{1,129},{65,193},{129,1},{193,65... | collective-permute-start | bytes 589832 | tf_op jit(solution)/shard_map/ppermute | solution.py:399
  14.8 12.4 %collective-permute-start.4 = (f32[384,128]{1,0:T(8,128)S(1)}, f32[384,128]{1,0:T(8,128)S(1)}, u32[]{:S(2)}, u32[]{:S(2)}) collective-permute-start(f32[384,128]{1,0:T(8,128)S(1)} %get-tuple-element.21), channel_id=1, source_target_pairs={{0,192},{64,0},{128,64},{192,128},{1,193},{65,1},{129,65},{193,129... | collective-permute-start | bytes 589832 | tf_op jit(solution)/shard_map/ppermute | solution.py:399
  59.0 5.2 %collective-permute-start.5 = (f32[384,128]{1,0:T(8,128)S(1)}, f32[384,128]{1,0:T(8,128)S(1)}, u32[]{:S(2)}, u32[]{:S(2)}) collective-permute-start(f32[384,128]{1,0:T(8,128)S(1)} %bitcast.3), channel_id=1, source_target_pairs={{0,16},{16,0},{1,17},{17,1},{2,18},{18,2},{3,19},{19,3},{4,20},{20... | collective-permute-start | bytes 589832 | tf_op jit(solution)/shard_map/ppermute | solution.py:405
